TPU v7x, 256 devices: a whole 4x4x8 slice. The times are simulated.
256 devices in a mesh: wide: 128 (over x, z_lo, y, core), narrow: 2 (over z_hi).
Axes of the slice: x: 4, y: 4, z: 8 (z_hi: 2, z_lo: 4; z = z_hi * 4 + z_lo), core: 2. Of those that a mesh axis runs over, the one named last changes fastest.
Arguments:
- tokens: bfloat16 [131072, 2048], P(('wide', 'narrow')), may hold values from -16 to 16
- slot_param: bfloat16 [2048, 512], P(None, 'wide'), may hold values from -4 to 4
- w_in: bfloat16 [128, 2048, 2048], P('wide', None, 'narrow'), may hold values from -0.125 to 0.125
- w_out: bfloat16 [128, 2048, 2048], P('wide', 'narrow'), may hold values from -0.125 to 0.125
Outputs:
- mixed: bfloat16 [131072, 2048], P(('wide', 'narrow'))
All inputs are finite; a program needn't handle non-finite values.
Results may differ from a plain program's by a relative error of at most 0.022.
Values may be sent and summed in bfloat16 or wider, within the bound.
No kernel may reach another device: no remote copies, remote signals or barrier semaphores. Data moves between devices by JAX's collectives and lax.ppermute only.
A program may use at most 64 MiB of HBM per device.

v0:
```python
import jax
import jax.numpy as jnp
from jax import lax
from jax.sharding import PartitionSpec as P

SLOTS = 4


logit_scale = 3.0
epsilon = 1e-06


def body(tokens, slot_param, w_in, w_out):
    param_f = slot_param.astype(jnp.float32)
    hat_local = (
        param_f * lax.rsqrt(jnp.sum(param_f * param_f, axis=0, keepdims=True) + epsilon)
    ).astype(jnp.bfloat16)
    hat_whole = lax.all_gather(hat_local, "wide", axis=1, tiled=True)
    logits = logit_scale * jnp.dot(tokens, hat_whole, preferred_element_type=jnp.float32)
    local_peak = jnp.max(logits, axis=0)
    col_peak = lax.pmax(local_peak, ("wide", "narrow"))
    exp_terms = jnp.exp(logits - col_peak[None, :])
    col_total = lax.psum(jnp.sum(exp_terms, axis=0), ("wide", "narrow"))
    dispatch = exp_terms.astype(jnp.bfloat16)
    slot_terms = lax.dot_general(
        dispatch, tokens, (((0,), (0,)), ((), ())), preferred_element_type=jnp.float32
    )
    group_slots = w_in.shape[0] * SLOTS
    summed = lax.psum(slot_terms.astype(jnp.bfloat16), "narrow").astype(jnp.float32)
    own_rows = lax.psum_scatter(summed, "wide", scatter_dimension=0, tiled=True)
    own_total = lax.dynamic_slice_in_dim(
        col_total, lax.axis_index("wide") * group_slots, group_slots, 0
    )
    slot_in = (own_rows / own_total[:, None]).astype(jnp.bfloat16)
    slot_in = slot_in.reshape(w_in.shape[0], SLOTS, slot_in.shape[1])
    hidden = jax.nn.gelu(
        jnp.einsum("esd,edf->esf", slot_in, w_in, preferred_element_type=jnp.float32)
    ).astype(jnp.bfloat16)
    half_terms = jnp.einsum("esf,efd->esd", hidden, w_out, preferred_element_type=jnp.float32)
    slot_out = lax.psum(
        half_terms.reshape(group_slots, half_terms.shape[2]).astype(jnp.bfloat16), "narrow"
    )
    row_peak = jnp.max(logits, axis=1, keepdims=True)
    row_terms = jnp.exp(logits - row_peak)
    combine_w = (row_terms / jnp.sum(row_terms, axis=1, keepdims=True)).astype(jnp.bfloat16)
    every_slot = lax.all_gather(slot_out, "wide", axis=0, tiled=True)
    mixed = jnp.dot(combine_w, every_slot, preferred_element_type=jnp.float32)
    return mixed.astype(jnp.bfloat16)


def solution(mesh):
    in_specs = (
        P(("wide", "narrow"), None),
        P(None, "wide"),
        P("wide", None, "narrow"),
        P("wide", "narrow", None),
    )
    out_specs = P(("wide", "narrow"), None)
    return jax.shard_map(body, mesh=mesh, in_specs=in_specs, out_specs=out_specs, check_vma=False)
```

profile of v0, /device:TPU:1, one launch (start us, length us, event | category | flops | bytes accessed | tf_op | source)
XLA Modules:
  0.0 1350.1 jit_solution(6553406468341898475)
XLA Ops:
  6.5 0.0 copy-start
  6.5 0.0 all-gather.5.cloned.1.call-start
  6.5 1.0 fusion.14
  7.5 1.4 fusion.38
  8.9 0.0 all-gather.5.cloned.1.call-update
  9.0 0.0 all-reduce.4.cloned.1.call-start
  9.0 200.9 %all-gather.5.cloned.1.call-done = bf16[128,4,2048]{2,1,0:T(4,128)(2,1)} async-done(((bf16[1,4,2048]{2,1,0:T(4,128)(2,1)}), bf16[128,4,2048]{2,1,0:T(4,128)(2,1)}) %all-gather.5.cloned.1.call-update) | async-done | bytes 2097168 | tf_op jit(solution)/shard_map/all_gather | solution.py:18
  209.9 3.9 reshape.38
  213.9 0.0 copy-done
  213.9 3.0 fusion.51
  216.8 75.4 %pmax.7 = f32[512]{0:T(512)S(1)} all-reduce(f32[512]{0:T(512)S(1)} %get-tuple-element.8), channel_id=1, replica_groups=mesh['wide'=128,'narrow'=2] {'wide','narrow'}, use_global_device_ids=true, to_apply=%region_4.0 | all-reduce | flops 512 | bytes 4096 | tf_op jit(solution)/shard_map/pmax | solution.py:21
  292.3 2.6 convolution_convert_fusion.1
  294.9 0.0 copy-start.1
  294.9 0.0 all-reduce.4.cloned.1.call-update
  294.9 0.0 all-gather.7.cloned.1.call-start
  295.0 0.6 copy-done.1
  295.6 0.7 dynamic-slice
  296.9 0.4 fusion.7
  297.3 96.8 %psum.22 = f32[512]{0:T(512)S(1)} all-reduce(f32[512]{0:T(512)S(1)} %get-tuple-element.6), channel_id=1, replica_groups=mesh['wide'=128,'narrow'=2] {'wide','narrow'}, use_global_device_ids=true, to_apply=%region_8.0 | all-reduce | flops 512 | bytes 4096 | tf_op jit(solution)/shard_map/psum | solution.py:23
  394.1 0.1 dynamic_slice.3
  394.2 20.3 %all-reduce.4.cloned.1.call-done = bf16[512,2048]{1,0:T(8,128)(2,1)} async-done(((bf16[512,2048]{1,0:T(8,128)(2,1)}), bf16[512,2048]{1,0:T(8,128)(2,1)}) %all-reduce.4.cloned.1.call-update) | async-done | bytes 2097168 | tf_op jit(solution)/shard_map/psum | solution.py:29
  414.5 699.7 %all-reduce.5 = f32[512,2048]{1,0:T(8,128)} all-reduce(bf16[512,2048]{1,0:T(8,128)(2,1)} %all-reduce.4.cloned.1.call-done), channel_id=2, replica_groups=mesh['wide'=128,'narrow'=2] {'wide'}, use_global_device_ids=true, to_apply=%region_6.0.clone | all-reduce | flops 1048576 | bytes 6291456
  1114.2 4.7 fusion.4
  1118.9 18.7 %psum.23 = bf16[4,2048]{1,0:T(4,128)(2,1)} all-reduce(bf16[4,2048]{1,0:T(4,128)(2,1)S(1)} %fusion.4), channel_id=1, replica_groups=mesh['wide'=128,'narrow'=2] {'narrow'}, use_global_device_ids=true, to_apply=%region_9.0 | all-reduce | flops 8192 | bytes 32768 | tf_op jit(solution)/shard_map/psum | solution.py:40
  1137.7 0.0 all-gather.7.cloned.1.call-update
  1137.7 197.6 %all-gather.7.cloned.1.call-done = bf16[128,4,2048]{2,1,0:T(4,128)(2,1)} async-done(((bf16[1,4,2048]{2,1,0:T(4,128)(2,1)}), bf16[128,4,2048]{2,1,0:T(4,128)(2,1)}) %all-gather.7.cloned.1.call-update) | async-done | bytes 2097168 | tf_op jit(solution)/shard_map/all_gather | solution.py:46
  1335.4 4.0 reshape.40
  1339.3 4.2 convolution_convert_fusion
  (1 shorter events, 0.0 us)
Async XLA Ops:
  6.5 207.3 %copy-start = (bf16[512,2048]{1,0:T(8,128)(2,1)S(1)}, bf16[512,2048]{1,0:T(8,128)(2,1)}, u32[]{:S(2)}) copy-start(bf16[512,2048]{1,0:T(8,128)(2,1)} %param.4) | copy-start | bytes 6291460
  6.5 203.4 %all-gather.5.cloned.1.call-start = ((), (), s32[]{:S(2)}) async-start(), calls=%async_computation.1 | async-start | bytes 2113536 | tf_op jit(solution)/shard_map/all_gather | solution.py:18
  9.0 405.5 %all-reduce.4.cloned.1.call-start = ((), (), s32[]{:S(2)}) async-start(), calls=%async_computation | async-start | bytes 4194304 | tf_op jit(solution)/shard_map/psum | solution.py:29
  294.9 0.7 copy-start.1
  294.9 1040.4 %all-gather.7.cloned.1.call-start = ((), (), s32[]{:S(2)}) async-start(), calls=%async_computation.2 | async-start | bytes 2113536 | tf_op jit(solution)/shard_map/all_gather | solution.py:46
Sparse Core Ops, SparseCore 0:
  9.2 200.6 all-gather.4
  295.0 119.3 all-reduce.3
  1137.8 197.4 all-gather.6
where the time goes:
time: 1350 us
  blocking collectives  891 us (66%)
  waiting for transfers between devices  419 us (31%)
  matrix products  14.5 us (1%)
  between operations  13.8 us (1%)
    unnamed x1, blocking collectives  700 us
    all_gather x1, waiting for transfers between devices, body(): hat_whole = lax.all_gather(hat_local, 'wide', axis=1, tiled=True)  201 us
    all_gather x1, waiting for transfers between devices, body(): every_slot = lax.all_gather(slot_out, 'wide', axis=0, tiled=True)  198 us
    psum x1, blocking collectives, body(): col_total = lax.psum(jnp.sum(exp_terms, axis=0), ('wide', 'narrow'))  96.8 us
    pmax x1, blocking collectives, body(): col_peak = lax.pmax(local_peak, ('wide', 'narrow'))  75.4 us
  transfers between devices with their start and end apart: 3, of which 3 were waited for; matrix products, arithmetic and copies ran while one was open for 0% of the time, Pallas kernels for 0%

commit v1 on v0

v1 whole, which is shorter than its diff:
```python
import jax
import jax.numpy as jnp
from jax import lax
from jax.sharding import Mesh, PartitionSpec as P

SLOTS = 4
logit_scale = 3.0
epsilon = 1e-06
AXES = ("x", "zl", "y", "core", "zh")
WIDE = ("x", "zl", "y", "core")
PLANE = ("x", "y")
RING = ("zl", "zh")
PAD = 128


def shift(n, k):
    return [(i, (i + k) % n) for i in range(n)]


def ring_shift(nl, nh, k):
    def place(z):
        return (z % nl) * nh + z // nl

    n = nl * nh
    return [(place(z), place((z + k) % n)) for z in range(n)]


def swap_core(a):
    return lax.ppermute(a, "core", shift(2, 1))


def to_plane(a):
    return lax.all_to_all(a, PLANE, split_axis=0, concat_axis=0, tiled=True)


def spread_plane(rows, n):
    whole = jnp.broadcast_to(rows[None], (n,) + rows.shape)
    return to_plane(whole.reshape(n * rows.shape[0], rows.shape[1]))


def pack(sums, peak, total):
    high = total.astype(jnp.bfloat16)
    low = (total - high.astype(jnp.float32)).astype(jnp.bfloat16)
    tail = jnp.concatenate(
        [peak[:, None], high[:, None], low[:, None], jnp.zeros((sums.shape[0], PAD - 3), jnp.bfloat16)], axis=1
    )
    return jnp.concatenate([sums.astype(jnp.bfloat16), tail], axis=1)


def merge(parts):
    d = parts.shape[2] - PAD
    sums = parts[:, :, :d].astype(jnp.float32)
    peaks = parts[:, :, d].astype(jnp.float32)
    totals = parts[:, :, d + 1].astype(jnp.float32) + parts[:, :, d + 2].astype(jnp.float32)
    peak = jnp.max(peaks, axis=0)
    weight = jnp.exp(peaks - peak[None])
    return (
        jnp.sum(sums * weight[:, :, None], axis=0),
        peak.astype(jnp.bfloat16),
        jnp.sum(totals * weight, axis=0),
    )


def make_body(size):
    nz, plane, ring = size["zl"], size["x"] * size["y"], size["zh"] * size["zl"]

    def body(tokens, slot_param, w_in, w_out):
        tokens_b = swap_core(tokens)
        param_f = slot_param.astype(jnp.float32)
        hat = (
            param_f * lax.rsqrt(jnp.sum(param_f * param_f, axis=0, keepdims=True) + epsilon)
        ).astype(jnp.bfloat16).T
        column = jnp.concatenate(
            [hat] + [lax.ppermute(hat, "zl", shift(nz, k)) for k in range(1, nz)], axis=0
        )
        hat_all = spread_plane(column, plane)
        nt = (((1,), (1,)), ((), ()))
        logits_a = logit_scale * lax.dot_general(tokens, hat_all, nt, preferred_element_type=jnp.float32)
        logits_b = logit_scale * lax.dot_general(tokens_b, hat_all, nt, preferred_element_type=jnp.float32)
        logits_c = swap_core(logits_b)
        peak = jnp.maximum(jnp.max(logits_a, axis=0), jnp.max(logits_b, axis=0)).astype(jnp.bfloat16)
        peak_f = peak.astype(jnp.float32)[None, :]
        exp_a = jnp.exp(logits_a - peak_f)
        exp_b = jnp.exp(logits_b - peak_f)
        total = jnp.sum(exp_a, axis=0) + jnp.sum(exp_b, axis=0)
        tn = (((0,), (0,)), ((), ()))
        sums = lax.dot_general(
            exp_a.astype(jnp.bfloat16), tokens, tn, preferred_element_type=jnp.float32
        ) + lax.dot_general(exp_b.astype(jnp.bfloat16), tokens_b, tn, preferred_element_type=jnp.float32)
        sent = pack(sums, peak, total)
        got = to_plane(sent).reshape(plane, sent.shape[0] // plane, sent.shape[1])
        sent = pack(*merge(got))
        blocks = [sent[SLOTS * k : SLOTS * (k + 1)] for k in range(nz)]
        got = jnp.stack(
            [blocks[0]] + [lax.ppermute(blocks[k % nz], RING, ring_shift(nz, 2, -k)) for k in range(1, ring)]
        )
        sums, _, total = merge(got)
        slot_in = (sums / total[:, None]).astype(jnp.bfloat16)
        hidden = jax.nn.gelu(jnp.dot(slot_in, w_in[0], preferred_element_type=jnp.float32)).astype(jnp.bfloat16)
        half = jnp.dot(hidden, w_out[0], preferred_element_type=jnp.float32).astype(jnp.bfloat16)
        halves = [half] + [lax.ppermute(half, RING, ring_shift(nz, 2, k)) for k in range(1, ring)]
        column = jnp.concatenate(
            [
                (halves[k].astype(jnp.float32) + halves[k + nz].astype(jnp.float32)).astype(jnp.bfloat16)
                for k in range(nz)
            ],
            axis=0,
        )
        out_a = spread_plane(column, plane)
        out_c = swap_core(out_a)
        row_peak = jnp.maximum(
            jnp.max(logits_a, axis=1, keepdims=True), jnp.max(logits_c, axis=1, keepdims=True)
        )
        row_a = jnp.exp(logits_a - row_peak)
        row_c = jnp.exp(logits_c - row_peak)
        row_sum = jnp.sum(row_a, axis=1, keepdims=True) + jnp.sum(row_c, axis=1, keepdims=True)
        mixed = jnp.dot(
            (row_a / row_sum).astype(jnp.bfloat16), out_a, preferred_element_type=jnp.float32
        ) + jnp.dot((row_c / row_sum).astype(jnp.bfloat16), out_c, preferred_element_type=jnp.float32)
        return mixed.astype(jnp.bfloat16)

    return body


def solution(mesh):
    fine = Mesh(mesh.devices.reshape(4, 4, 4, 2, 2), AXES)
    in_specs = (P(AXES, None), P(None, WIDE), P(WIDE, None, "zh"), P(WIDE, "zh", None))
    return jax.shard_map(
        make_body(dict(fine.shape)), mesh=fine, in_specs=in_specs, out_specs=P(AXES, None), check_vma=False
    )
```

time: 1350 us -> 134 us (0.10)
  blocking collectives: 891 us -> 56.6 us
  waiting for transfers between devices: 419 us -> 7.42 us
  starting transfers between devices: 0.09 us -> 45 us
    unnamed x1 -> x0, blocking collectives: 700 us -> none
    all_gather x2 -> x0, waiting for transfers between devices: 399 us -> none  [the longest x1 201 us: body(): hat_whole = lax.all_gather(hat_local, 'wide', axis=1, tiled=True)]
    psum x2 -> x0, blocking collectives: 116 us -> none  [the longest x1 96.8 us: body(): col_total = lax.psum(jnp.sum(exp_terms, axis=0), ('wide', 'narrow'))]
    pmax x1 -> x0, blocking collectives: 75.4 us -> none  [body(): col_peak = lax.pmax(local_peak, ('wide', 'narrow'))]
    all_to_all x0 -> x3, blocking collectives: none -> 56.6 us  [to_plane(): return lax.all_to_all(a, PLANE, split_axis=0, concat_axis=0, tiled=True)]
    ppermute x0 -> x20, starting transfers between devices: none -> 45 us  [the longest x3 14.4 us: swap_core(): return lax.ppermute(a, 'core', shift(2, 1))]
    psum x1 -> x0, waiting for transfers between devices: 20.3 us -> none  [body(): lax.psum(slot_terms.astype(jnp.bfloat16), 'narrow').astype(jnp.float32)]
  transfers between devices with their start and end apart: 3 -> 20, of which waited for: 3 -> 6; matrix products, arithmetic and copies ran while one was open for 0% -> 7% of each run, Pallas kernels for 0% -> 0%
where the time goes in v1:
time: 134 us
  blocking collectives  56.6 us (42%)
  starting transfers between devices  45 us (34%)
  matrix products  14.3 us (11%)
  waiting for transfers between devices  7.42 us (6%)
  local copies, waits for them, and re-layouts  5.29 us (4%)
  other arithmetic  4.61 us (3%)
    all_to_all x3, blocking collectives, to_plane(): return lax.all_to_all(a, PLANE, split_axis=0, concat_axis=0, tiled=True)  56.6 us
    ppermute x3, starting transfers between devices, swap_core(): return lax.ppermute(a, 'core', shift(2, 1))  14.4 us
    ppermute x7, starting transfers between devices, body(): lax.ppermute(blocks[k % nz], RING, ring_shift(nz, 2, -k))  14.2 us
    ppermute x7, starting transfers between devices, body(): lax.ppermute(half, RING, ring_shift(nz, 2, k))  13.4 us
    dot_general x1, matrix products, body(): jnp.dot(hidden, w_out[0], preferred_element_type=jnp.float32)  4.77 us
    ppermute x3, waiting for transfers between devices, body(): lax.ppermute(hat, 'zl', shift(nz, k))  4.02 us
    dot_general x1, matrix products, body(): lax.dot_general(exp_b.astype(jnp.bfloat16), tokens_b, tn, preferred_eleme...  3.54 us
    ppermute x3, starting transfers between devices, body(): lax.ppermute(hat, 'zl', shift(nz, k))  3.02 us
  transfers between devices with their start and end apart: 20, of which 6 were waited for; matrix products, arithmetic and copies ran while one was open for 7% of the time, Pallas kernels for 0%

profile of v1, /device:TPU:1, one launch (start us, length us, event | category | flops | bytes accessed | tf_op | source)
XLA Modules:
  0.0 133.6 jit_solution(10592330998670222602)
XLA Ops:
  0.0 3.2 %collective-permute-start.3 = (bf16[512,2048]{1,0:T(8,128)(2,1)}, bf16[512,2048]{1,0:T(8,128)(2,1)S(1)}, u32[]{:S(2)}, u32[]{:S(2)}) collective-permute-start(bf16[512,2048]{1,0:T(8,128)(2,1)} %param.4), channel_id=1, source_target_pairs={{0,2},{2,0},{1,3},{3,1},{4,6},{6,4},{5,7},{7,5},{8,10},{10,8},{9,1... | collective-permute-start | bytes 6291464 | tf_op jit(solution)/shard_map/ppermute | solution.py:29
  3.2 0.8 fusion.25
  4.1 0.8 fusion.43
  4.9 2.6 %collective-permute-start.2 = (bf16[4,2048]{1,0:T(4,128)(2,1)S(1)}, bf16[4,2048]{1,0:T(4,128)(2,1)S(1)}, u32[]{:S(2)}, u32[]{:S(2)}) collective-permute-start(bf16[4,2048]{1,0:T(4,128)(2,1)S(1)} %fusion.43), channel_id=1, source_target_pairs={{0,48},{16,0},{32,16},{48,32},{1,49},{17,1},{33,17},{49,33},{2,50}... | collective-permute-start | bytes 49160 | tf_op jit(solution)/shard_map/ppermute | solution.py:74
  7.5 0.0 collective-permute-start.1
  7.5 0.4 collective-permute-start
  7.9 0.5 collective-permute-done.2
  8.4 2.6 %collective-permute-done.1 = bf16[4,2048]{1,0:T(4,128)(2,1)S(1)} collective-permute-done((bf16[4,2048]{1,0:T(4,128)(2,1)S(1)}, bf16[4,2048]{1,0:T(4,128)(2,1)S(1)}, u32[]{:S(2)}, u32[]{:S(2)}) %collective-permute-start.1) | collective-permute-done | bytes 16416 | tf_op jit(solution)/shard_map/ppermute | solution.py:74
  11.0 0.9 collective-permute-done
  12.0 0.1 broadcast_in_dim.8
  12.1 21.4 %all_to_all.24 = bf16[16,16,2048]{2,1,0:T(8,128)(2,1)S(1)} all-to-all(bf16[16,16,2048]{2,1,0:T(8,128)(2,1)S(1)} %broadcast_in_dim.8), channel_id=1, replica_groups=mesh['x'=4,'zl'=4,'y'=4,'core'=2,'zh'=2] {'x','y'}, dimensions={0} | all-to-all | bytes 2097152 | tf_op jit(solution)/shard_map/all_to_all | solution.py:33
  33.5 0.8 fusion.60
  34.4 0.0 collective-permute-done.3
  34.4 0.0 copy-start
  34.4 1.6 %fusion.64 = (bf16[256]{0:T(256)(128)(2,1)S(1)}, f32[256,512]{1,0:T(8,128)}) fusion(bf16[256,2048]{1,0:T(8,128)(2,1)S(1)} %bitcast.68, bf16[512,2048]{1,0:T(8,128)(2,1)S(1)} %collective-permute-done.3), kind=kOutput, calls=%fused_computation.90 | convolution fusion | flops 537132800 | bytes 3670528 | tf_op jit(solution)/shard_map/dot_general | solution.py:79
  36.0 3.2 %collective-permute-start.4 = (f32[512,256]{0,1:T(8,128)}, f32[512,256]{0,1:T(8,128)S(1)}, u32[]{:S(2)}, u32[]{:S(2)}) collective-permute-start(f32[512,256]{0,1:T(8,128)} %bitcast.2), channel_id=1, source_target_pairs={{0,2},{2,0},{1,3},{3,1},{4,6},{6,4},{5,7},{7,5},{8,10},{10,8},{9,1... | collective-permute-start | bytes 1572872 | tf_op jit(solution)/shard_map/ppermute | solution.py:29
  39.2 0.8 fusion.16
  39.9 0.2 convert_element_type.256
  40.2 1.3 fusion.13
  41.4 3.5 %fusion.4 = bf16[256,2048]{1,0:T(8,128)(2,1)} fusion(f32[256,2048]{1,0:T(8,128)S(1)} %fusion.16, bf16[512,2048]{1,0:T(8,128)(2,1)} %copy-done, f32[256]{0:T(256)S(1)} %get-tuple-element.14, f32[256,512]{1,0:T(8,128)} %get-tuple-element.27), kind=kOutput, calls=%fused_computation.6 | convolution fusion | flops 538181632 | bytes 5768192 | tf_op jit(solution)/shard_map/dot_general | solution.py:89
  45.0 0.1 reduce_max.67
  45.1 0.2 fusion.9
  45.3 0.1 add.78
  45.4 0.2 copy.76
  45.6 0.2 copy.75
  45.8 2.4 %concatenate.17 = bf16[16,16,2176]{2,1,0:T(8,128)(2,1)S(1)} concatenate(bf16[16,16,2048]{2,1,0:T(8,128)(2,1)} %bitcast.64, bf16[16,16,1]{2,1,0:T(8,128)(2,1)S(1)} %convert_element_type.256, bf16[16,16,1]{2,1,0:T(8,128)(2,1)S(1)} %copy.75, bf16[16,16,1]{2,1,0:T(8,128)(2,1)S(1)} %copy.76, bf16[16,16,125]{2,1,0:T(8,128)(2,1)S(1)} %broadcast_in_dim.9), dimensions={2} | concatenate | bytes 2228224 | tf_op jit(solution)/shard_map/concatenate | solution.py:47
  48.2 20.5 %all_to_all.25 = bf16[16,16,2176]{2,1,0:T(8,128)(2,1)S(1)} all-to-all(bf16[16,16,2176]{2,1,0:T(8,128)(2,1)S(1)} %concatenate.17), channel_id=1, replica_groups=mesh['x'=4,'zl'=4,'y'=4,'core'=2,'zh'=2] {'x','y'}, dimensions={0} | all-to-all | bytes 2228224 | tf_op jit(solution)/shard_map/all_to_all | solution.py:33
  68.6 0.1 fusion.62
  68.8 0.2 copy.97
  68.9 0.2 copy.96
  69.1 0.2 copy.98
  69.4 0.1 copy.83
  69.5 0.1 copy.84
  69.6 0.1 copy.82
  69.7 0.3 multiply_reduce_fusion
  69.9 0.1 concatenate.18
  70.1 4.6 %collective-permute-start.8 = (bf16[4,2176]{1,0:T(4,128)(2,1)S(1)}, bf16[4,2176]{1,0:T(4,128)(2,1)S(1)}, u32[]{:S(2)}, u32[]{:S(2)}) collective-permute-start(bf16[4,2176]{1,0:T(4,128)(2,1)S(1)} %get-tuple-element.20), channel_id=1, source_target_pairs={{0,1},{16,17},{32,33},{48,49},{1,0},{17,16},{33,32},{49,48},{2,3},... | collective-permute-start | bytes 52232 | tf_op jit(solution)/shard_map/ppermute | solution.py:95
  74.7 0.5 collective-permute-start.7
  75.3 4.2 %collective-permute-start.10 = (bf16[4,2176]{1,0:T(4,128)(2,1)S(1)}, bf16[4,2176]{1,0:T(4,128)(2,1)S(1)}, u32[]{:S(2)}, u32[]{:S(2)}) collective-permute-start(bf16[4,2176]{1,0:T(4,128)(2,1)S(1)} %get-tuple-element.23), channel_id=1, source_target_pairs={{0,32},{16,48},{32,1},{48,17},{1,33},{17,49},{33,0},{49,16},{2,34}... | collective-permute-start | bytes 52232 | tf_op jit(solution)/shard_map/ppermute | solution.py:95
  79.5 0.0 collective-permute-start.6
  79.5 0.0 collective-permute-done.8
  79.5 0.9 collective-permute-start.9
  80.4 3.9 %collective-permute-start.5 = (bf16[4,2176]{1,0:T(4,128)(2,1)S(1)}, bf16[4,2176]{1,0:T(4,128)(2,1)S(1)}, u32[]{:S(2)}, u32[]{:S(2)}) collective-permute-start(bf16[4,2176]{1,0:T(4,128)(2,1)S(1)} %get-tuple-element.24), channel_id=1, source_target_pairs={{0,49},{16,0},{32,16},{48,32},{1,48},{17,1},{33,17},{49,33},{2,51}... | collective-permute-start | bytes 52232 | tf_op jit(solution)/shard_map/ppermute | solution.py:95
  84.5 0.6 collective-permute-done.9
  85.2 0.5 stack.35
  85.7 0.1 slice_reduce_fusion
  85.8 0.2 convert_reduce_fusion
  86.0 0.2 multiply_reduce_fusion.1
  86.1 0.4 copy.95
  86.5 0.2 multiply_reduce_fusion.2
  86.7 4.8 %fusion.5 = bf16[4,2048]{1,0:T(4,128)(2,1)S(1)} fusion(bf16[1,1024,2048]{2,1,0:T(8,128)(2,1)} %param.7, bf16[1,2048,1024]{2,1,0:T(8,128)(2,1)} %param.6, f32[4,2048]{0,1:T(8,128)S(1)} %copy.95, f32[4]{0:T(128)S(1)} %multiply_reduce_fusion.2), kind=kOutput, calls=%fused_computation.7 | convolution fusion | flops 33615872 | bytes 8437776 | tf_op jit(solution)/shard_map/dot_general | solution.py:100
  91.4 3.8 %collective-permute-start.12 = (bf16[4,2048]{1,0:T(4,128)(2,1)S(1)}, bf16[4,2048]{1,0:T(4,128)(2,1)S(1)}, u32[]{:S(2)}, u32[]{:S(2)}) collective-permute-start(bf16[4,2048]{1,0:T(4,128)(2,1)S(1)} %fusion.5), channel_id=1, source_target_pairs={{0,1},{16,17},{32,33},{48,49},{1,0},{17,16},{33,32},{49,48},{2,3},... | collective-permute-start | bytes 49160 | tf_op jit(solution)/shard_map/ppermute | solution.py:101
  95.2 2.1 %collective-permute-start.17 = (bf16[4,2048]{1,0:T(4,128)(2,1)S(1)}, bf16[4,2048]{1,0:T(4,128)(2,1)S(1)}, u32[]{:S(2)}, u32[]{:S(2)}) collective-permute-start(bf16[4,2048]{1,0:T(4,128)(2,1)S(1)} %fusion.5), channel_id=1, source_target_pairs={{0,48},{16,1},{32,17},{48,33},{1,49},{17,0},{33,16},{49,32},{2,50}... | collective-permute-start | bytes 49160 | tf_op jit(solution)/shard_map/ppermute | solution.py:101
  97.4 2.6 %collective-permute-start.16 = (bf16[4,2048]{1,0:T(4,128)(2,1)S(1)}, bf16[4,2048]{1,0:T(4,128)(2,1)S(1)}, u32[]{:S(2)}, u32[]{:S(2)}) collective-permute-start(bf16[4,2048]{1,0:T(4,128)(2,1)S(1)} %fusion.5), channel_id=1, source_target_pairs={{0,33},{16,49},{32,0},{48,16},{1,32},{17,48},{33,1},{49,17},{2,35}... | collective-permute-start | bytes 49160 | tf_op jit(solution)/shard_map/ppermute | solution.py:101
  100.0 2.1 %collective-permute-start.14 = (bf16[4,2048]{1,0:T(4,128)(2,1)S(1)}, bf16[4,2048]{1,0:T(4,128)(2,1)S(1)}, u32[]{:S(2)}, u32[]{:S(2)}) collective-permute-start(bf16[4,2048]{1,0:T(4,128)(2,1)S(1)} %fusion.5), channel_id=1, source_target_pairs={{0,17},{16,33},{32,49},{48,0},{1,16},{17,32},{33,48},{49,1},{2,19}... | collective-permute-start | bytes 49160 | tf_op jit(solution)/shard_map/ppermute | solution.py:101
  102.1 2.8 %collective-permute-start.13 = (bf16[4,2048]{1,0:T(4,128)(2,1)S(1)}, bf16[4,2048]{1,0:T(4,128)(2,1)S(1)}, u32[]{:S(2)}, u32[]{:S(2)}) collective-permute-start(bf16[4,2048]{1,0:T(4,128)(2,1)S(1)} %fusion.5), channel_id=1, source_target_pairs={{0,16},{16,32},{32,48},{48,1},{1,17},{17,33},{33,49},{49,0},{2,18}... | collective-permute-start | bytes 49160 | tf_op jit(solution)/shard_map/ppermute | solution.py:101
  104.9 1.4 %collective-permute-done.13 = bf16[4,2048]{1,0:T(4,128)(2,1)S(1)} collective-permute-done((bf16[4,2048]{1,0:T(4,128)(2,1)S(1)}, bf16[4,2048]{1,0:T(4,128)(2,1)S(1)}, u32[]{:S(2)}, u32[]{:S(2)}) %collective-permute-start.13) | collective-permute-done | bytes 16416 | tf_op jit(solution)/shard_map/ppermute | solution.py:101
  106.4 0.1 broadcast_in_dim.11
  106.5 14.8 %all_to_all.26 = bf16[16,16,2048]{2,1,0:T(8,128)(2,1)S(1)} all-to-all(bf16[16,16,2048]{2,1,0:T(8,128)(2,1)S(1)} %broadcast_in_dim.11), channel_id=1, replica_groups=mesh['x'=4,'zl'=4,'y'=4,'core'=2,'zh'=2] {'x','y'}, dimensions={0} | all-to-all | bytes 2097152 | tf_op jit(solution)/shard_map/all_to_all | solution.py:33
  121.2 8.0 %collective-permute-start.19 = (bf16[256,2048]{1,0:T(8,128)(2,1)S(1)}, bf16[256,2048]{1,0:T(8,128)(2,1)S(1)}, u32[]{:S(2)}, u32[]{:S(2)}) collective-permute-start(bf16[256,2048]{1,0:T(8,128)(2,1)S(1)} %bitcast.65), channel_id=1, source_target_pairs={{0,2},{2,0},{1,3},{3,1},{4,6},{6,4},{5,7},{7,5},{8,10},{10,8},{9,1... | collective-permute-start | bytes 3145736 | tf_op jit(solution)/shard_map/ppermute | solution.py:29
  129.2 0.1 fusion.10
  129.3 0.8 fusion.18
  130.1 1.4 %collective-permute-done.19 = bf16[256,2048]{1,0:T(8,128)(2,1)S(1)} collective-permute-done((bf16[256,2048]{1,0:T(8,128)(2,1)S(1)}, bf16[256,2048]{1,0:T(8,128)(2,1)S(1)}, u32[]{:S(2)}, u32[]{:S(2)}) %collective-permute-start.19) | collective-permute-done | bytes 1048608 | tf_op jit(solution)/shard_map/ppermute | solution.py:29
  131.5 2.1 %add_convert_fusion = bf16[512,2048]{1,0:T(8,128)(2,1)} fusion(f32[512,2048]{1,0:T(8,128)S(1)} %fusion.18, bf16[256,2048]{1,0:T(8,128)(2,1)S(1)} %collective-permute-done.19, f32[512,256]{0,1:T(8,128)S(1)} %collective-permute-done.4, f32[512]{0:T(512)S(1)} %add.75, f32[512]{0:T(512)S(1)} %max.24), kind=kOutput, calls=%fused_computation.4 | convolution fusion | flops 539361280 | bytes 7868416 | tf_op jit(solution)/shard_map/dot_general | solution.py:119
  (47 shorter events, 0.6 us)
Async XLA Ops:
  0.0 33.5 %copy-start.1 = (bf16[512,2048]{1,0:T(8,128)(2,1)S(1)}, bf16[512,2048]{1,0:T(8,128)(2,1)}, u32[]{:S(2)}) copy-start(bf16[512,2048]{1,0:T(8,128)(2,1)} %param.4) | copy-start | bytes 6291460
  0.0 34.4 %collective-permute-start.3 = (bf16[512,2048]{1,0:T(8,128)(2,1)}, bf16[512,2048]{1,0:T(8,128)(2,1)S(1)}, u32[]{:S(2)}, u32[]{:S(2)}) collective-permute-start(bf16[512,2048]{1,0:T(8,128)(2,1)} %param.4), channel_id=1, source_target_pairs={{0,2},{2,0},{1,3},{3,1},{4,6},{6,4},{5,7},{7,5},{8,10},{10,8},{9,1... | collective-permute-start | bytes 6291464 | tf_op jit(solution)/shard_map/ppermute | solution.py:29
  4.9 3.5 %collective-permute-start.2 = (bf16[4,2048]{1,0:T(4,128)(2,1)S(1)}, bf16[4,2048]{1,0:T(4,128)(2,1)S(1)}, u32[]{:S(2)}, u32[]{:S(2)}) collective-permute-start(bf16[4,2048]{1,0:T(4,128)(2,1)S(1)} %fusion.43), channel_id=1, source_target_pairs={{0,48},{16,0},{32,16},{48,32},{1,49},{17,1},{33,17},{49,33},{2,50}... | collective-permute-start | bytes 49160 | tf_op jit(solution)/shard_map/ppermute | solution.py:74
  7.5 3.5 %collective-permute-start.1 = (bf16[4,2048]{1,0:T(4,128)(2,1)S(1)}, bf16[4,2048]{1,0:T(4,128)(2,1)S(1)}, u32[]{:S(2)}, u32[]{:S(2)}) collective-permute-start(bf16[4,2048]{1,0:T(4,128)(2,1)S(1)} %fusion.43), channel_id=1, source_target_pairs={{0,32},{16,48},{32,0},{48,16},{1,33},{17,49},{33,1},{49,17},{2,34}... | collective-permute-start | bytes 49160 | tf_op jit(solution)/shard_map/ppermute | solution.py:74
  7.5 4.4 %collective-permute-start = (bf16[4,2048]{1,0:T(4,128)(2,1)S(1)}, bf16[4,2048]{1,0:T(4,128)(2,1)S(1)}, u32[]{:S(2)}, u32[]{:S(2)}) collective-permute-start(bf16[4,2048]{1,0:T(4,128)(2,1)S(1)} %fusion.43), channel_id=1, source_target_pairs={{0,16},{16,32},{32,48},{48,0},{1,17},{17,33},{33,49},{49,1},{2,18}... | collective-permute-start | bytes 49160 | tf_op jit(solution)/shard_map/ppermute | solution.py:74
  34.4 5.6 %copy-start = (bf16[512,2048]{1,0:T(8,128)(2,1)}, bf16[512,2048]{1,0:T(8,128)(2,1)S(1)}, u32[]{:S(2)}) copy-start(bf16[512,2048]{1,0:T(8,128)(2,1)S(1)} %collective-permute-done.3) | copy-start | bytes 6291460
  36.0 9.0 %collective-permute-start.4 = (f32[512,256]{0,1:T(8,128)}, f32[512,256]{0,1:T(8,128)S(1)}, u32[]{:S(2)}, u32[]{:S(2)}) collective-permute-start(f32[512,256]{0,1:T(8,128)} %bitcast.2), channel_id=1, source_target_pairs={{0,2},{2,0},{1,3},{3,1},{4,6},{6,4},{5,7},{7,5},{8,10},{10,8},{9,1... | collective-permute-start | bytes 1572872 | tf_op jit(solution)/shard_map/ppermute | solution.py:29
  70.1 9.4 %collective-permute-start.8 = (bf16[4,2176]{1,0:T(4,128)(2,1)S(1)}, bf16[4,2176]{1,0:T(4,128)(2,1)S(1)}, u32[]{:S(2)}, u32[]{:S(2)}) collective-permute-start(bf16[4,2176]{1,0:T(4,128)(2,1)S(1)} %get-tuple-element.20), channel_id=1, source_target_pairs={{0,1},{16,17},{32,33},{48,49},{1,0},{17,16},{33,32},{49,48},{2,3},... | collective-permute-start | bytes 52232 | tf_op jit(solution)/shard_map/ppermute | solution.py:95
  74.7 5.6 %collective-permute-start.11 = (bf16[4,2176]{1,0:T(4,128)(2,1)S(1)}, bf16[4,2176]{1,0:T(4,128)(2,1)S(1)}, u32[]{:S(2)}, u32[]{:S(2)}) collective-permute-start(bf16[4,2176]{1,0:T(4,128)(2,1)S(1)} %get-tuple-element.22), channel_id=1, source_target_pairs={{0,16},{16,32},{32,48},{48,1},{1,17},{17,33},{33,49},{49,0},{2,18}... | collective-permute-start | bytes 52232 | tf_op jit(solution)/shard_map/ppermute | solution.py:95
  74.7 9.6 %collective-permute-start.7 = (bf16[4,2176]{1,0:T(4,128)(2,1)S(1)}, bf16[4,2176]{1,0:T(4,128)(2,1)S(1)}, u32[]{:S(2)}, u32[]{:S(2)}) collective-permute-start(bf16[4,2176]{1,0:T(4,128)(2,1)S(1)} %get-tuple-element.22), channel_id=1, source_target_pairs={{0,17},{16,33},{32,49},{48,0},{1,16},{17,32},{33,48},{49,1},{2,19}... | collective-permute-start | bytes 52232 | tf_op jit(solution)/shard_map/ppermute | solution.py:95
  75.3 9.1 %collective-permute-start.10 = (bf16[4,2176]{1,0:T(4,128)(2,1)S(1)}, bf16[4,2176]{1,0:T(4,128)(2,1)S(1)}, u32[]{:S(2)}, u32[]{:S(2)}) collective-permute-start(bf16[4,2176]{1,0:T(4,128)(2,1)S(1)} %get-tuple-element.23), channel_id=1, source_target_pairs={{0,32},{16,48},{32,1},{48,17},{1,33},{17,49},{33,0},{49,16},{2,34}... | collective-permute-start | bytes 52232 | tf_op jit(solution)/shard_map/ppermute | solution.py:95
  79.5 5.0 %collective-permute-start.6 = (bf16[4,2176]{1,0:T(4,128)(2,1)S(1)}, bf16[4,2176]{1,0:T(4,128)(2,1)S(1)}, u32[]{:S(2)}, u32[]{:S(2)}) collective-permute-start(bf16[4,2176]{1,0:T(4,128)(2,1)S(1)} %get-tuple-element.23), channel_id=1, source_target_pairs={{0,33},{16,49},{32,0},{48,16},{1,32},{17,48},{33,1},{49,17},{2,35}... | collective-permute-start | bytes 52232 | tf_op jit(solution)/shard_map/ppermute | solution.py:95
  79.5 5.6 %collective-permute-start.9 = (bf16[4,2176]{1,0:T(4,128)(2,1)S(1)}, bf16[4,2176]{1,0:T(4,128)(2,1)S(1)}, u32[]{:S(2)}, u32[]{:S(2)}) collective-permute-start(bf16[4,2176]{1,0:T(4,128)(2,1)S(1)} %get-tuple-element.24), channel_id=1, source_target_pairs={{0,48},{16,1},{32,17},{48,33},{1,49},{17,0},{33,16},{49,32},{2,50}... | collective-permute-start | bytes 52232 | tf_op jit(solution)/shard_map/ppermute | solution.py:95
  80.4 4.8 %collective-permute-start.5 = (bf16[4,2176]{1,0:T(4,128)(2,1)S(1)}, bf16[4,2176]{1,0:T(4,128)(2,1)S(1)}, u32[]{:S(2)}, u32[]{:S(2)}) collective-permute-start(bf16[4,2176]{1,0:T(4,128)(2,1)S(1)} %get-tuple-element.24), channel_id=1, source_target_pairs={{0,49},{16,0},{32,16},{48,32},{1,48},{17,1},{33,17},{49,33},{2,51}... | collective-permute-start | bytes 52232 | tf_op jit(solution)/shard_map/ppermute | solution.py:95
  91.4 8.6 %collective-permute-start.12 = (bf16[4,2048]{1,0:T(4,128)(2,1)S(1)}, bf16[4,2048]{1,0:T(4,128)(2,1)S(1)}, u32[]{:S(2)}, u32[]{:S(2)}) collective-permute-start(bf16[4,2048]{1,0:T(4,128)(2,1)S(1)} %fusion.5), channel_id=1, source_target_pairs={{0,1},{16,17},{32,33},{48,49},{1,0},{17,16},{33,32},{49,48},{2,3},... | collective-permute-start | bytes 49160 | tf_op jit(solution)/shard_map/ppermute | solution.py:101
  95.2 6.9 %collective-permute-start.18 = (bf16[4,2048]{1,0:T(4,128)(2,1)S(1)}, bf16[4,2048]{1,0:T(4,128)(2,1)S(1)}, u32[]{:S(2)}, u32[]{:S(2)}) collective-permute-start(bf16[4,2048]{1,0:T(4,128)(2,1)S(1)} %fusion.5), channel_id=1, source_target_pairs={{0,49},{16,0},{32,16},{48,32},{1,48},{17,1},{33,17},{49,33},{2,51}... | collective-permute-start | bytes 49160 | tf_op jit(solution)/shard_map/ppermute | solution.py:101
  95.2 9.6 %collective-permute-start.17 = (bf16[4,2048]{1,0:T(4,128)(2,1)S(1)}, bf16[4,2048]{1,0:T(4,128)(2,1)S(1)}, u32[]{:S(2)}, u32[]{:S(2)}) collective-permute-start(bf16[4,2048]{1,0:T(4,128)(2,1)S(1)} %fusion.5), channel_id=1, source_target_pairs={{0,48},{16,1},{32,17},{48,33},{1,49},{17,0},{33,16},{49,32},{2,50}... | collective-permute-start | bytes 49160 | tf_op jit(solution)/shard_map/ppermute | solution.py:101
  97.4 7.5 %collective-permute-start.16 = (bf16[4,2048]{1,0:T(4,128)(2,1)S(1)}, bf16[4,2048]{1,0:T(4,128)(2,1)S(1)}, u32[]{:S(2)}, u32[]{:S(2)}) collective-permute-start(bf16[4,2048]{1,0:T(4,128)(2,1)S(1)} %fusion.5), channel_id=1, source_target_pairs={{0,33},{16,49},{32,0},{48,16},{1,32},{17,48},{33,1},{49,17},{2,35}... | collective-permute-start | bytes 49160 | tf_op jit(solution)/shard_map/ppermute | solution.py:101
  100.0 4.9 %collective-permute-start.15 = (bf16[4,2048]{1,0:T(4,128)(2,1)S(1)}, bf16[4,2048]{1,0:T(4,128)(2,1)S(1)}, u32[]{:S(2)}, u32[]{:S(2)}) collective-permute-start(bf16[4,2048]{1,0:T(4,128)(2,1)S(1)} %fusion.5), channel_id=1, source_target_pairs={{0,32},{16,48},{32,1},{48,17},{1,33},{17,49},{33,0},{49,16},{2,34}... | collective-permute-start | bytes 49160 | tf_op jit(solution)/shard_map/ppermute | solution.py:101
  100.0 4.9 %collective-permute-start.14 = (bf16[4,2048]{1,0:T(4,128)(2,1)S(1)}, bf16[4,2048]{1,0:T(4,128)(2,1)S(1)}, u32[]{:S(2)}, u32[]{:S(2)}) collective-permute-start(bf16[4,2048]{1,0:T(4,128)(2,1)S(1)} %fusion.5), channel_id=1, source_target_pairs={{0,17},{16,33},{32,49},{48,0},{1,16},{17,32},{33,48},{49,1},{2,19}... | collective-permute-start | bytes 49160 | tf_op jit(solution)/shard_map/ppermute | solution.py:101
  102.1 4.2 %collective-permute-start.13 = (bf16[4,2048]{1,0:T(4,128)(2,1)S(1)}, bf16[4,2048]{1,0:T(4,128)(2,1)S(1)}, u32[]{:S(2)}, u32[]{:S(2)}) collective-permute-start(bf16[4,2048]{1,0:T(4,128)(2,1)S(1)} %fusion.5), channel_id=1, source_target_pairs={{0,16},{16,32},{32,48},{48,1},{1,17},{17,33},{33,49},{49,0},{2,18}... | collective-permute-start | bytes 49160 | tf_op jit(solution)/shard_map/ppermute | solution.py:101
  121.2 10.3 %collective-permute-start.19 = (bf16[256,2048]{1,0:T(8,128)(2,1)S(1)}, bf16[256,2048]{1,0:T(8,128)(2,1)S(1)}, u32[]{:S(2)}, u32[]{:S(2)}) collective-permute-start(bf16[256,2048]{1,0:T(8,128)(2,1)S(1)} %bitcast.65), channel_id=1, source_target_pairs={{0,2},{2,0},{1,3},{3,1},{4,6},{6,4},{5,7},{7,5},{8,10},{10,8},{9,1... | collective-permute-start | bytes 3145736 | tf_op jit(solution)/shard_map/ppermute | solution.py:29

commit v2 on v0

v2 whole, which is shorter than its diff:
```python
import jax
import jax.numpy as jnp
from jax import lax
from jax.experimental import pallas as pl
from jax.experimental.pallas import tpu as pltpu
from jax.sharding import Mesh, PartitionSpec as P

SLOTS = 4
logit_scale = 3.0
epsilon = 1e-06
AXES = ("x", "zl", "y", "core", "zh")
WIDE = ("x", "zl", "y", "core")
PLANE = ("x", "y")
RING = ("zl", "zh")
PAD = 128
TILE = 512
MIB = 1 << 20
NT = (((1,), (1,)), ((), ()))
VMEM = pl.BlockSpec(memory_space=pltpu.VMEM)
SMEM = pl.BlockSpec(memory_space=pltpu.SMEM)
ANY = pl.BlockSpec(memory_space=pl.ANY)
HBM = pl.BlockSpec(memory_space=pltpu.HBM)
DMA = pltpu.SemaphoreType.DMA


def shift(n, k):
    return [(i, (i + k) % n) for i in range(n)]


def swap_core(a):
    return lax.ppermute(a, "core", shift(2, 1))


def exchange(a, axes):
    return lax.all_to_all(a, axes, split_axis=0, concat_axis=0, tiled=True)


def call(kernel, out, *args, limit=8, specs=None, out_specs=None, scratch=(), flops=0):
    specs = specs or [VMEM] * len(args)
    spaces = {id(VMEM): pltpu.VMEM, id(HBM): pltpu.HBM}
    args = [
        pltpu.with_memory_space_constraint(a, spaces[id(s)]) if id(s) in spaces else a
        for a, s in zip(args, specs)
    ]
    return pl.pallas_call(
        kernel,
        out_shape=out,
        in_specs=specs,
        out_specs=out_specs or jax.tree.map(lambda _: VMEM, out),
        scratch_shapes=list(scratch),
        compiler_params=pltpu.CompilerParams(vmem_limit_bytes=limit * MIB),
        cost_estimate=pl.CostEstimate(flops=flops, bytes_accessed=1 << 20, transcendentals=0),
    )(*args)


def tail_of(peak, total):
    lane = lax.broadcasted_iota(jnp.int32, (peak.shape[0], PAD), 1)
    high = total.astype(jnp.bfloat16).astype(jnp.float32)
    low = total - high
    tail = jnp.where(lane == 0, peak, jnp.where(lane == 1, high, jnp.where(lane == 2, low, 0.0)))
    return tail.astype(jnp.bfloat16)


def fetch_kernel(*refs):
    n = len(refs) // 3
    copies = [pltpu.make_async_copy(refs[i], refs[n + i], refs[2 * n + i]) for i in range(n)]
    for c in copies:
        c.start()
    for c in copies:
        c.wait()


def hat_kernel(*refs):
    out = refs[-1]
    p = jnp.concatenate([r[...].astype(jnp.float32) for r in refs[:-1]], axis=0)
    hat = (p * lax.rsqrt(jnp.sum(p * p, axis=1, keepdims=True) + epsilon)).astype(jnp.bfloat16)
    for i in range(out.shape[0]):
        out[i] = hat


def slots_kernel(tok_a, tok_b, hat, sent, log_a, log_b):
    d = tok_a.shape[1]
    parts = []
    for tok, out in ((tok_b, log_b), (tok_a, log_a)):
        logits = logit_scale * lax.dot_general(hat[...], tok[...], NT, preferred_element_type=jnp.float32)
        out[...] = logits
        peak = jnp.max(logits, axis=1, keepdims=True).astype(jnp.bfloat16).astype(jnp.float32)
        terms = jnp.exp(logits - peak)
        parts.append((tok, terms.astype(jnp.bfloat16), peak, jnp.sum(terms, axis=1, keepdims=True)))
    peak = jnp.maximum(parts[0][2], parts[1][2])
    scale = [jnp.exp(p[2] - peak) for p in parts]
    sent[:, d:] = tail_of(peak, sum(p[3] * s for p, s in zip(parts, scale)))
    for j in range(0, d, TILE):
        cols = slice(j, j + TILE)
        sums = [jnp.dot(p[1], p[0][:, cols], preferred_element_type=jnp.float32) * s for p, s in zip(parts, scale)]
        sent[:, cols] = (sums[0] + sums[1]).astype(jnp.bfloat16)


def weights_of(tails):
    peak = tails[0][:, 0:1]
    for t in tails[1:]:
        peak = jnp.maximum(peak, t[:, 0:1])
    weights = [jnp.exp(t[:, 0:1] - peak) for t in tails]
    total = sum(w * (t[:, 1:2] + t[:, 2:3]) for w, t in zip(weights, tails))
    return peak, weights, total


def merge_kernel(place, got, after, sent):
    n, rows, wide = got.shape
    d = wide - PAD
    nz = rows // SLOTS
    copies = sent.shape[0] // nz
    peak, weights, total = weights_of([got[i, :, d:].astype(jnp.float32) for i in range(n)])

    def put(block, lo, hi):
        for k in range(nz):
            z = lax.rem(place[0] - k + nz, nz)
            for h in range(copies):
                sent[z * copies + h, :, lo:hi] = block[SLOTS * k : SLOTS * (k + 1)]

    put(tail_of(peak, total), d, wide)
    for j in range(0, d, TILE):
        acc = got[0, :, j : j + TILE].astype(jnp.float32) * weights[0]
        for i in range(1, n):
            acc += got[i, :, j : j + TILE].astype(jnp.float32) * weights[i]
        put(acc.astype(jnp.bfloat16), j, j + TILE)


def expert_kernel(got, w_in, w_out, out, in_v, out_v, sems):
    cuts = sems.shape[1]
    copies = []
    for j, (src, dst) in enumerate(((w_in, in_v), (w_out, out_v))):
        step = dst.shape[0] // cuts
        for i in range(cuts):
            rows = pl.ds(i * step, step)
            copies.append(pltpu.make_async_copy(src.at[0, rows, :], dst.at[rows, :], sems.at[j, i]))
            copies[-1].start()
    n, rows, wide = got.shape
    d = wide - PAD
    _, weights, total = weights_of([got[i, :, d:].astype(jnp.float32) for i in range(n)])
    acc = got[0, :, :d].astype(jnp.float32) * weights[0]
    for i in range(1, n):
        acc += got[i, :, :d].astype(jnp.float32) * weights[i]
    row = (acc / total).astype(jnp.bfloat16)
    for j, held in enumerate((in_v, out_v)):
        step = held.shape[0] // cuts
        acc = jnp.zeros((rows, held.shape[1]), jnp.float32)
        for i in range(cuts):
            copies[j * cuts + i].wait()
            acc += jnp.dot(
                row[:, i * step : (i + 1) * step],
                held[i * step : (i + 1) * step, :],
                preferred_element_type=jnp.float32,
            )
        row = (jax.nn.gelu(acc) if j == 0 else acc).astype(jnp.bfloat16)
    for i in range(out.shape[0]):
        out[i] = row


def column_kernel(place, got, out):
    nz = out.shape[1] // SLOTS
    copies = got.shape[0] // nz
    parts = []
    for k in range(nz):
        z = lax.rem(place[0] - k + nz, nz)
        acc = got[z * copies].astype(jnp.float32)
        for h in range(1, copies):
            acc += got[z * copies + h].astype(jnp.float32)
        parts.append(acc)
    column = jnp.concatenate(parts, axis=0).astype(jnp.bfloat16)
    for i in range(out.shape[0]):
        out[i] = column


def combine_kernel(log_a, log_c, out_a, out_c):
    peak = jnp.maximum(jnp.max(log_a[...], axis=0, keepdims=True), jnp.max(log_c[...], axis=0, keepdims=True))
    terms = [jnp.exp(r[...] - peak) for r in (log_a, log_c)]
    total = sum(jnp.sum(t, axis=0, keepdims=True) for t in terms)
    for t, out in zip(terms, (out_a, out_c)):
        out[...] = jnp.transpose(t / total).astype(jnp.bfloat16)


def mixed_kernel(w_a, w_c, out_a, out_c, mixed, held, sems):
    blocks, pieces = sems.shape
    step = w_a.shape[0] // blocks
    cut = step // pieces
    copies = []
    for i in range(blocks):
        r = pl.ds(i * step, step)
        acc = jnp.dot(w_a[r, :], out_a[...], preferred_element_type=jnp.float32)
        acc += jnp.dot(w_c[r, :], out_c[...], preferred_element_type=jnp.float32)
        held[r, :] = acc.astype(jnp.bfloat16)
        for j in range(pieces):
            c = pl.ds(i * step + j * cut, cut)
            copies.append(pltpu.make_async_copy(held.at[c, :], mixed.at[c, :], sems.at[i, j]))
            copies[-1].start()
    for c in copies:
        c.wait()


def make_body(size):
    nz, plane, ring = size["zl"], size["x"] * size["y"], size["zh"] * size["zl"]

    def body(tokens, slot_param, w_in, w_out):
        n_tok, d = tokens.shape
        rows = nz * SLOTS
        bf, f32 = jnp.bfloat16, jnp.float32
        S = jax.ShapeDtypeStruct
        place = lax.axis_index("zl").astype(jnp.int32).reshape(1)
        param = slot_param.T
        param_v, tokens_a = call(
            fetch_kernel, [pltpu.VMEM(param.shape, bf), pltpu.VMEM(tokens.shape, bf)], param, tokens,
            specs=[HBM] * 2, scratch=[DMA(())] * 2, flops=1 << 31,
        )
        blocks = [param_v] + [lax.ppermute(param, "zl", shift(nz, k)) for k in range(1, nz)]
        tokens_b = swap_core(tokens)
        own = plane * rows
        hat = exchange(call(hat_kernel, S((plane, rows, d), bf), *blocks), PLANE)
        sent, log_a, log_b = call(
            slots_kernel,
            [S((own, d + PAD), bf), S((own, n_tok), f32), S((own, n_tok), f32)],
            tokens_a, tokens_b, hat.reshape(own, d), flops=8 * own * n_tok * d,
        )
        got = exchange(sent.reshape(plane, rows, d + PAD), PLANE)
        log_c = swap_core(log_b)
        w_a, w_c = call(combine_kernel, [S((n_tok, own), bf)] * 2, log_a, log_c, flops=1 << 26)
        sent = call(
            merge_kernel, S((ring, SLOTS, d + PAD), bf), place, got, w_a, specs=[SMEM, VMEM, ANY]
        )
        got = exchange(sent, RING)
        half = call(
            expert_kernel, S((ring, SLOTS, d), bf), got, w_in, w_out, limit=14,
            specs=[VMEM, HBM, HBM],
            scratch=[pltpu.VMEM(w_in.shape[1:], bf), pltpu.VMEM(w_out.shape[1:], bf), DMA((2, 4))],
            flops=4 * SLOTS * d * w_in.shape[2]
        )
        got = exchange(half, RING)
        sent = call(column_kernel, S((plane, rows, d), bf), place, got, specs=[SMEM, VMEM])
        out_a = exchange(sent, PLANE).reshape(own, d)
        out_c = swap_core(out_a)
        mixed = call(
            mixed_kernel, S((n_tok, d), bf), w_a, w_c, out_a, out_c, out_specs=ANY, limit=8,
            scratch=[pltpu.VMEM((n_tok, d), bf), DMA((2, 4))], flops=4 * n_tok * own * d,
        )
        return mixed

    return body


def solution(mesh):
    fine = Mesh(mesh.devices.reshape(4, 4, 4, 2, 2), AXES)
    in_specs = (P(AXES, None), P(None, WIDE), P(WIDE, None, "zh"), P(WIDE, "zh", None))
    return jax.shard_map(
        make_body(dict(fine.shape)), mesh=fine, in_specs=in_specs, out_specs=P(AXES, None), check_vma=False
    )
```

time: 1350 us -> 108 us (0.08)
  blocking collectives: 891 us -> 61.3 us
  waiting for transfers between devices: 419 us -> 13.8 us
  starting transfers between devices: 0.09 us -> 19.8 us
  matrix products: 14.5 us -> 0 us
  between operations: 13.8 us -> 0.08 us
    unnamed x1 -> x0, blocking collectives: 700 us -> none
    all_gather x2 -> x0, waiting for transfers between devices: 399 us -> none  [the longest x1 201 us: body(): hat_whole = lax.all_gather(hat_local, 'wide', axis=1, tiled=True)]
    psum x2 -> x0, blocking collectives: 116 us -> none  [the longest x1 96.8 us: body(): col_total = lax.psum(jnp.sum(exp_terms, axis=0), ('wide', 'narrow'))]
    pmax x1 -> x0, blocking collectives: 75.4 us -> none  [body(): col_peak = lax.pmax(local_peak, ('wide', 'narrow'))]
    all_to_all x0 -> x4, blocking collectives: none -> 61.3 us  [exchange(): return lax.all_to_all(a, axes, split_axis=0, concat_axis=0, tiled=True)]
    psum x1 -> x0, waiting for transfers between devices: 20.3 us -> none  [body(): lax.psum(slot_terms.astype(jnp.bfloat16), 'narrow').astype(jnp.float32)]
    ppermute x0 -> x6, starting transfers between devices: none -> 16.1 us  [the longest x3 12.5 us: swap_core(): return lax.ppermute(a, 'core', shift(2, 1))]
    dot_general x4 -> x0, matrix products: 14.5 us -> none  [the longest x1 4.74 us: body(): jnp.einsum('esf,efd->esd', hidden, w_out, preferred_element_type=jnp.floa...]
  transfers between devices with their start and end apart: 3 -> 7, of which waited for: 3 -> 4; matrix products, arithmetic and copies ran while one was open for 0% -> 0% of each run, Pallas kernels for 0% -> 2%
where the time goes in v2:
time: 108 us; the launch traced here: 107 us
  blocking collectives  61.3 us (57%)
  starting transfers between devices  19.8 us (18%)
  waiting for transfers between devices  13.8 us (13%)
  Pallas kernels  12.2 us (11%)
    all_to_all x4, blocking collectives, exchange(): return lax.all_to_all(a, axes, split_axis=0, concat_axis=0, tiled=True)  61.3 us
    ppermute x3, starting transfers between devices, swap_core(): return lax.ppermute(a, 'core', shift(2, 1))  12.5 us
    pallas_call x8, Pallas kernels, call(): pl.pallas_call(kernel, out_shape=out, in_specs=specs, out_specs=out_specs...  12.2 us
    all_to_all x1, waiting for transfers between devices, exchange(): return lax.all_to_all(a, axes, split_axis=0, concat_axis=0, tiled=True)  9.55 us
    ppermute x3, waiting for transfers between devices, swap_core(): return lax.ppermute(a, 'core', shift(2, 1))  3.83 us
    all_to_all x1, starting transfers between devices, exchange(): return lax.all_to_all(a, axes, split_axis=0, concat_axis=0, tiled=True)  3.7 us
    ppermute x3, starting transfers between devices, body(): lax.ppermute(param, 'zl', shift(nz, k))  3.62 us
  transfers between devices with their start and end apart: 7, of which 4 were waited for; matrix products, arithmetic and copies ran while one was open for 0% of the time, Pallas kernels for 2%

profile of v2, /device:TPU:1, one launch (start us, length us, event | category | flops | bytes accessed | tf_op | source)
XLA Modules:
  0.0 107.2 jit_solution(11270946024922606378)
XLA Ops:
  0.0 3.2 %collective-permute-start = (bf16[512,2048]{1,0:T(8,128)(2,1)}, bf16[512,2048]{1,0:T(8,128)(2,1)S(1)}, u32[]{:S(2)}, u32[]{:S(2)}) collective-permute-start(bf16[512,2048]{1,0:T(8,128)(2,1)} %refs_1_.1), channel_id=1, source_target_pairs={{0,2},{2,0},{1,3},{3,1},{4,6},{6,4},{5,7},{7,5},{8,10},{10,8},{9,1... | collective-permute-start | bytes 6291464 | tf_op jit(solution)/shard_map/ppermute | solution.py:31
  3.2 0.0 collective-permute-start.1
  3.2 2.9 %collective-permute-start.2 = (bf16[4,2048]{1,0:T(4,128)(2,1)}, bf16[4,2048]{1,0:T(4,128)(2,1)S(1)}, u32[]{:S(2)}, u32[]{:S(2)}) collective-permute-start(bf16[4,2048]{1,0:T(4,128)(2,1)} %bitcast.9), channel_id=1, source_target_pairs={{0,32},{16,48},{32,0},{48,16},{1,33},{17,49},{33,1},{49,17},{2,34}... | collective-permute-start | bytes 49160 | tf_op jit(solution)/shard_map/ppermute | solution.py:215
  6.1 0.7 collective-permute-start.3
  6.9 1.6 %shard_map.46 = (bf16[4,2048]{1,0:T(4,128)(2,1)S(1)}, bf16[512,2048]{1,0:T(8,128)(2,1)S(1)}) custom-call(bf16[4,2048]{1,0:T(4,128)(2,1)} %bitcast.11, bf16[512,2048]{1,0:T(8,128)(2,1)} %refs_1_.1), custom_call_target="tpu_custom_call" | custom-call | flops 2147483648 | bytes 1048576 | tf_op jit(solution)/shard_map/pallas_call | solution.py:45
  8.5 0.0 collective-permute-done.1.refs_1_
  8.5 0.0 collective-permute-done.2.refs_2_
  8.5 0.4 collective-permute-done.3.refs_3_
  8.9 0.2 shard_map.47
  9.1 21.5 %all_to_all.25 = bf16[16,16,2048]{2,1,0:T(8,128)(2,1)S(1)} all-to-all(bf16[16,16,2048]{2,1,0:T(8,128)(2,1)S(1)} %shard_map.47), channel_id=1, replica_groups=mesh['x'=4,'zl'=4,'y'=4,'core'=2,'zh'=2] {'x','y'}, dimensions={0} | all-to-all | bytes 2097152 | tf_op jit(solution)/shard_map/all_to_all | solution.py:35
  30.6 0.0 collective-permute-done.tok_b
  30.6 3.5 %shard_map.48 = (bf16[256,2176]{1,0:T(8,128)(2,1)}, f32[256,512]{1,0:T(8,128)S(1)}, f32[256,512]{1,0:T(8,128)S(1)}) custom-call(bf16[512,2048]{1,0:T(8,128)(2,1)S(1)} %get-tuple-element.12.tok_a, bf16[512,2048]{1,0:T(8,128)(2,1)S(1)} %collective-permute-done.tok_b, bf16[256,2048]{1,0:T(8,128)(2,1)S(1)} %bitcast.7), custom_call_target="tpu_custom_call" | custom-call | flops 2147483648 | bytes 1048576 | tf_op jit(solution)/shard_map/pallas_call | solution.py:45
  34.1 3.7 %all-to-all-start.1 = ((bf16[16,16,2176]{2,1,0:T(8,128)(2,1)}), bf16[16,16,2176]{2,1,0:T(8,128)(2,1)S(1)}, u32[]{:S(2)}, u32[]{:S(2)}) async-start(bf16[16,16,2176]{2,1,0:T(8,128)(2,1)} %bitcast.3), calls=%async_computation.1 | async-start | bytes 2228224 | tf_op jit(solution)/shard_map/all_to_all | solution.py:35
  37.8 3.2 %collective-permute-start.4 = (f32[256,512]{1,0:T(8,128)S(1)}, f32[256,512]{1,0:T(8,128)S(1)}, u32[]{:S(2)}, u32[]{:S(2)}) collective-permute-start(f32[256,512]{1,0:T(8,128)S(1)} %get-tuple-element.15), channel_id=1, source_target_pairs={{0,2},{2,0},{1,3},{3,1},{4,6},{6,4},{5,7},{7,5},{8,10},{10,8},{9,1... | collective-permute-start | bytes 1572872 | tf_op jit(solution)/shard_map/ppermute | solution.py:31
  41.0 1.5 %collective-permute-done.4.log_c = f32[256,512]{1,0:T(8,128)S(1)} collective-permute-done((f32[256,512]{1,0:T(8,128)S(1)}, f32[256,512]{1,0:T(8,128)S(1)}, u32[]{:S(2)}, u32[]{:S(2)}) %collective-permute-start.4) | collective-permute-done | bytes 524320 | tf_op jit(solution)/shard_map/ppermute | solution.py:31
  42.5 0.5 shard_map.49
  43.0 9.5 %all-to-all-done.1.got = bf16[16,16,2176]{2,1,0:T(8,128)(2,1)S(1)} async-done(((bf16[16,16,2176]{2,1,0:T(8,128)(2,1)}), bf16[16,16,2176]{2,1,0:T(8,128)(2,1)S(1)}, u32[]{:S(2)}, u32[]{:S(2)}) %all-to-all-start.1) | async-done | bytes 1114144 | tf_op jit(solution)/shard_map/all_to_all | solution.py:35
  52.5 0.4 shard_map.50
  52.9 12.9 %all_to_all.26.got = bf16[8,4,2176]{2,1,0:T(4,128)(2,1)S(1)} all-to-all(bf16[8,4,2176]{2,1,0:T(4,128)(2,1)S(1)} %shard_map.50), channel_id=1, replica_groups=mesh['x'=4,'zl'=4,'y'=4,'core'=2,'zh'=2] {'zl','zh'}, dimensions={0} | all-to-all | bytes 278528 | tf_op jit(solution)/shard_map/all_to_all | solution.py:35
  65.9 3.7 %shard_map.51 = bf16[8,4,2048]{2,1,0:T(4,128)(2,1)S(1)} custom-call(bf16[8,4,2176]{2,1,0:T(4,128)(2,1)S(1)} %all_to_all.26.got, bf16[1,2048,1024]{2,1,0:T(8,128)(2,1)} %w_in.1, bf16[1,1024,2048]{2,1,0:T(8,128)(2,1)} %w_out.1), custom_call_target="tpu_custom_call" | custom-call | flops 33554432 | bytes 1048576 | tf_op jit(solution)/shard_map/pallas_call | solution.py:45
  69.6 9.4 %all_to_all.27.got = bf16[8,4,2048]{2,1,0:T(4,128)(2,1)S(1)} all-to-all(bf16[8,4,2048]{2,1,0:T(4,128)(2,1)S(1)} %shard_map.51), channel_id=1, replica_groups=mesh['x'=4,'zl'=4,'y'=4,'core'=2,'zh'=2] {'zl','zh'}, dimensions={0} | all-to-all | bytes 262144 | tf_op jit(solution)/shard_map/all_to_all | solution.py:35
  79.0 0.1 shard_map.52
  79.1 17.5 %all_to_all.28 = bf16[16,16,2048]{2,1,0:T(8,128)(2,1)S(1)} all-to-all(bf16[16,16,2048]{2,1,0:T(8,128)(2,1)S(1)} %shard_map.52), channel_id=1, replica_groups=mesh['x'=4,'zl'=4,'y'=4,'core'=2,'zh'=2] {'x','y'}, dimensions={0} | all-to-all | bytes 2097152 | tf_op jit(solution)/shard_map/all_to_all | solution.py:35
  96.6 6.0 %collective-permute-start.5 = (bf16[256,2048]{1,0:T(8,128)(2,1)S(1)}, bf16[256,2048]{1,0:T(8,128)(2,1)S(1)}, u32[]{:S(2)}, u32[]{:S(2)}) collective-permute-start(bf16[256,2048]{1,0:T(8,128)(2,1)S(1)} %bitcast.5), channel_id=1, source_target_pairs={{0,2},{2,0},{1,3},{3,1},{4,6},{6,4},{5,7},{7,5},{8,10},{10,8},{9,1... | collective-permute-start | bytes 3145736 | tf_op jit(solution)/shard_map/ppermute | solution.py:31
  102.6 2.3 %collective-permute-done.5.out_c = bf16[256,2048]{1,0:T(8,128)(2,1)S(1)} collective-permute-done((bf16[256,2048]{1,0:T(8,128)(2,1)S(1)}, bf16[256,2048]{1,0:T(8,128)(2,1)S(1)}, u32[]{:S(2)}, u32[]{:S(2)}) %collective-permute-start.5) | collective-permute-done | bytes 1048608 | tf_op jit(solution)/shard_map/ppermute | solution.py:31
  104.9 2.3 %shard_map.53 = bf16[512,2048]{1,0:T(8,128)(2,1)} custom-call(bf16[512,256]{1,0:T(8,128)(2,1)S(1)} %get-tuple-element.16.after.w_a, bf16[512,256]{1,0:T(8,128)(2,1)S(1)} %get-tuple-element.17.w_c, bf16[256,2048]{1,0:T(8,128)(2,1)S(1)} %bitcast.6, bf16[256,2048]{1,0:T(8,128)(2,1)S(1)} %collective-permute-done.5.out_c), custom_call_target="tpu_custom_call" | custom-call | flops 1073741824 | bytes 1048576 | tf_op jit(solution)/shard_map/pallas_call | solution.py:45
Async XLA Ops:
  0.0 30.6 %collective-permute-start = (bf16[512,2048]{1,0:T(8,128)(2,1)}, bf16[512,2048]{1,0:T(8,128)(2,1)S(1)}, u32[]{:S(2)}, u32[]{:S(2)}) collective-permute-start(bf16[512,2048]{1,0:T(8,128)(2,1)} %refs_1_.1), channel_id=1, source_target_pairs={{0,2},{2,0},{1,3},{3,1},{4,6},{6,4},{5,7},{7,5},{8,10},{10,8},{9,1... | collective-permute-start | bytes 6291464 | tf_op jit(solution)/shard_map/ppermute | solution.py:31
  3.2 5.3 %collective-permute-start.1 = (bf16[4,2048]{1,0:T(4,128)(2,1)}, bf16[4,2048]{1,0:T(4,128)(2,1)S(1)}, u32[]{:S(2)}, u32[]{:S(2)}) collective-permute-start(bf16[4,2048]{1,0:T(4,128)(2,1)} %bitcast.8), channel_id=1, source_target_pairs={{0,16},{16,32},{32,48},{48,0},{1,17},{17,33},{33,49},{49,1},{2,18}... | collective-permute-start | bytes 49160 | tf_op jit(solution)/shard_map/ppermute | solution.py:215
  3.2 5.3 %collective-permute-start.2 = (bf16[4,2048]{1,0:T(4,128)(2,1)}, bf16[4,2048]{1,0:T(4,128)(2,1)S(1)}, u32[]{:S(2)}, u32[]{:S(2)}) collective-permute-start(bf16[4,2048]{1,0:T(4,128)(2,1)} %bitcast.9), channel_id=1, source_target_pairs={{0,32},{16,48},{32,0},{48,16},{1,33},{17,49},{33,1},{49,17},{2,34}... | collective-permute-start | bytes 49160 | tf_op jit(solution)/shard_map/ppermute | solution.py:215
  6.1 2.8 %collective-permute-start.3 = (bf16[4,2048]{1,0:T(4,128)(2,1)}, bf16[4,2048]{1,0:T(4,128)(2,1)S(1)}, u32[]{:S(2)}, u32[]{:S(2)}) collective-permute-start(bf16[4,2048]{1,0:T(4,128)(2,1)} %bitcast.10), channel_id=1, source_target_pairs={{0,48},{16,0},{32,16},{48,32},{1,49},{17,1},{33,17},{49,33},{2,50}... | collective-permute-start | bytes 49160 | tf_op jit(solution)/shard_map/ppermute | solution.py:215
  34.1 18.5 %all-to-all-start.1 = ((bf16[16,16,2176]{2,1,0:T(8,128)(2,1)}), bf16[16,16,2176]{2,1,0:T(8,128)(2,1)S(1)}, u32[]{:S(2)}, u32[]{:S(2)}) async-start(bf16[16,16,2176]{2,1,0:T(8,128)(2,1)} %bitcast.3), calls=%async_computation.1 | async-start | bytes 2228224 | tf_op jit(solution)/shard_map/all_to_all | solution.py:35
  37.8 4.7 %collective-permute-start.4 = (f32[256,512]{1,0:T(8,128)S(1)}, f32[256,512]{1,0:T(8,128)S(1)}, u32[]{:S(2)}, u32[]{:S(2)}) collective-permute-start(f32[256,512]{1,0:T(8,128)S(1)} %get-tuple-element.15), channel_id=1, source_target_pairs={{0,2},{2,0},{1,3},{3,1},{4,6},{6,4},{5,7},{7,5},{8,10},{10,8},{9,1... | collective-permute-start | bytes 1572872 | tf_op jit(solution)/shard_map/ppermute | solution.py:31
  96.6 8.3 %collective-permute-start.5 = (bf16[256,2048]{1,0:T(8,128)(2,1)S(1)}, bf16[256,2048]{1,0:T(8,128)(2,1)S(1)}, u32[]{:S(2)}, u32[]{:S(2)}) collective-permute-start(bf16[256,2048]{1,0:T(8,128)(2,1)S(1)} %bitcast.5), channel_id=1, source_target_pairs={{0,2},{2,0},{1,3},{3,1},{4,6},{6,4},{5,7},{7,5},{8,10},{10,8},{9,1... | collective-permute-start | bytes 3145736 | tf_op jit(solution)/shard_map/ppermute | solution.py:31

commit v3 on v2

--- a/solution.py
+++ b/solution.py
@@ -14,6 +14,7 @@
 RING = ("zl", "zh")
 PAD = 128
 TILE = 512
+SUM_TILE = 1024
 MIB = 1 << 20
 NT = (((1,), (1,)), ((), ()))
 VMEM = pl.BlockSpec(memory_space=pltpu.VMEM)
@@ -78,6 +79,18 @@
         out[i] = hat
 
 
+def pieces_kernel(whole, after, *refs):
+    parts, sems = refs[:-1], refs[-1]
+    step = parts[0].shape[0]
+    copies = [
+        pltpu.make_async_copy(whole.at[0, pl.ds(i * step, step), :], p, sems.at[i]) for i, p in enumerate(parts)
+    ]
+    for c in copies:
+        c.start()
+    for c in copies:
+        c.wait()
+
+
 def slots_kernel(tok_a, tok_b, hat, sent, log_a, log_b):
     d = tok_a.shape[1]
     parts = []
@@ -90,8 +103,8 @@
     peak = jnp.maximum(parts[0][2], parts[1][2])
     scale = [jnp.exp(p[2] - peak) for p in parts]
     sent[:, d:] = tail_of(peak, sum(p[3] * s for p, s in zip(parts, scale)))
-    for j in range(0, d, TILE):
-        cols = slice(j, j + TILE)
+    for j in range(0, d, SUM_TILE):
+        cols = slice(j, j + SUM_TILE)
         sums = [jnp.dot(p[1], p[0][:, cols], preferred_element_type=jnp.float32) * s for p, s in zip(parts, scale)]
         sent[:, cols] = (sums[0] + sums[1]).astype(jnp.bfloat16)
 
@@ -126,15 +139,15 @@
         put(acc.astype(jnp.bfloat16), j, j + TILE)
 
 
-def expert_kernel(got, w_in, w_out, out, in_v, out_v, sems):
-    cuts = sems.shape[1]
+def expert_kernel(got, *refs):
+    first, (w_out, out, out_v, sems) = refs[:-4], refs[-4:]
+    cuts = sems.shape[0]
+    step = out_v.shape[0] // cuts
     copies = []
-    for j, (src, dst) in enumerate(((w_in, in_v), (w_out, out_v))):
-        step = dst.shape[0] // cuts
-        for i in range(cuts):
-            rows = pl.ds(i * step, step)
-            copies.append(pltpu.make_async_copy(src.at[0, rows, :], dst.at[rows, :], sems.at[j, i]))
-            copies[-1].start()
+    for i in range(cuts * 4):
+        r = pl.ds(i * (step // 4), step // 4)
+        copies.append(pltpu.make_async_copy(w_out.at[0, r, :], out_v.at[r, :], sems.at[i // 4, i % 4]))
+        copies[-1].start()
     n, rows, wide = got.shape
     d = wide - PAD
     _, weights, total = weights_of([got[i, :, d:].astype(jnp.float32) for i in range(n)])
@@ -142,17 +155,18 @@
     for i in range(1, n):
         acc += got[i, :, :d].astype(jnp.float32) * weights[i]
     row = (acc / total).astype(jnp.bfloat16)
-    for j, held in enumerate((in_v, out_v)):
-        step = held.shape[0] // cuts
-        acc = jnp.zeros((rows, held.shape[1]), jnp.float32)
-        for i in range(cuts):
-            copies[j * cuts + i].wait()
-            acc += jnp.dot(
-                row[:, i * step : (i + 1) * step],
-                held[i * step : (i + 1) * step, :],
-                preferred_element_type=jnp.float32,
-            )
-        row = (jax.nn.gelu(acc) if j == 0 else acc).astype(jnp.bfloat16)
+    acc = jnp.zeros((rows, w_out.shape[1]), jnp.float32)
+    for i, w in enumerate(first):
+        k = w.shape[0]
+        acc += jnp.dot(row[:, i * k : (i + 1) * k], w[...], preferred_element_type=jnp.float32)
+    row = jax.nn.gelu(acc).astype(jnp.bfloat16)
+    acc = jnp.zeros((rows, d), jnp.float32)
+    for i in range(cuts):
+        for c in copies[4 * i : 4 * i + 4]:
+            c.wait()
+        r = slice(i * step, (i + 1) * step)
+        acc += jnp.dot(row[:, r], out_v[r, :], preferred_element_type=jnp.float32)
+    row = acc.astype(jnp.bfloat16)
     for i in range(out.shape[0]):
         out[i] = row
 
@@ -180,20 +194,20 @@
         out[...] = jnp.transpose(t / total).astype(jnp.bfloat16)
 
 
-def mixed_kernel(w_a, w_c, out_a, out_c, mixed, held, sems):
-    blocks, pieces = sems.shape
-    step = w_a.shape[0] // blocks
-    cut = step // pieces
+def first_kernel(weight, rows, acc):
+    acc[...] = jnp.dot(weight[...], rows[...], preferred_element_type=jnp.float32)
+
+
+def mixed_kernel(acc, weight, rows, mixed, held, sems):
+    blocks = sems.shape[0]
+    step = weight.shape[0] // blocks
     copies = []
     for i in range(blocks):
         r = pl.ds(i * step, step)
-        acc = jnp.dot(w_a[r, :], out_a[...], preferred_element_type=jnp.float32)
-        acc += jnp.dot(w_c[r, :], out_c[...], preferred_element_type=jnp.float32)
-        held[r, :] = acc.astype(jnp.bfloat16)
-        for j in range(pieces):
-            c = pl.ds(i * step + j * cut, cut)
-            copies.append(pltpu.make_async_copy(held.at[c, :], mixed.at[c, :], sems.at[i, j]))
-            copies[-1].start()
+        total = acc[r, :] + jnp.dot(weight[r, :], rows[...], preferred_element_type=jnp.float32)
+        held[r, :] = total.astype(jnp.bfloat16)
+        copies.append(pltpu.make_async_copy(held.at[r, :], mixed.at[r, :], sems.at[i]))
+        copies[-1].start()
     for c in copies:
         c.wait()
 
@@ -224,23 +238,28 @@
         got = exchange(sent.reshape(plane, rows, d + PAD), PLANE)
         log_c = swap_core(log_b)
         w_a, w_c = call(combine_kernel, [S((n_tok, own), bf)] * 2, log_a, log_c, flops=1 << 26)
+        cut = (w_in.shape[1] // 4, w_in.shape[2])
+        held = call(
+            pieces_kernel, [pltpu.VMEM(cut, bf)] * 4, w_in, w_a, specs=[HBM, ANY], scratch=[DMA((4,))], flops=1 << 31
+        )
         sent = call(
-            merge_kernel, S((ring, SLOTS, d + PAD), bf), place, got, w_a, specs=[SMEM, VMEM, ANY]
+            merge_kernel, S((ring, SLOTS, d + PAD), bf), place, got, held[3], specs=[SMEM, VMEM, ANY]
         )
         got = exchange(sent, RING)
         half = call(
-            expert_kernel, S((ring, SLOTS, d), bf), got, w_in, w_out, limit=14,
-            specs=[VMEM, HBM, HBM],
-            scratch=[pltpu.VMEM(w_in.shape[1:], bf), pltpu.VMEM(w_out.shape[1:], bf), DMA((2, 4))],
+            expert_kernel, S((ring, SLOTS, d), bf), got, *held, w_out, limit=8,
+            specs=[VMEM] * 5 + [HBM],
+            scratch=[pltpu.VMEM(w_out.shape[1:], bf), DMA((4, 4))],
             flops=4 * SLOTS * d * w_in.shape[2]
         )
         got = exchange(half, RING)
         sent = call(column_kernel, S((plane, rows, d), bf), place, got, specs=[SMEM, VMEM])
         out_a = exchange(sent, PLANE).reshape(own, d)
         out_c = swap_core(out_a)
+        acc = call(first_kernel, pltpu.VMEM((n_tok, d), f32), w_a, out_a, flops=2 * n_tok * own * d)
         mixed = call(
-            mixed_kernel, S((n_tok, d), bf), w_a, w_c, out_a, out_c, out_specs=ANY, limit=8,
-            scratch=[pltpu.VMEM((n_tok, d), bf), DMA((2, 4))], flops=4 * n_tok * own * d,
+            mixed_kernel, S((n_tok, d), bf), acc, w_c, out_c, out_specs=ANY,
+            scratch=[pltpu.VMEM((n_tok, d), bf), DMA((4,))], flops=2 * n_tok * own * d,
         )
         return mixed
 

time: 108 us -> 107 us (level)
  waiting for transfers between devices: 13.8 us -> 10.4 us
  local copies, waits for them, and re-layouts: 0 us -> 2.69 us
  Pallas kernels: 12.2 us -> 14 us
    all_to_all x1, waiting for transfers between devices: 9.55 us -> 4.62 us  [exchange(): return lax.all_to_all(a, axes, split_axis=0, concat_axis=0, tiled=True)]
    unnamed x0 -> x12, local copies, waits for them, and re-layouts: none -> 2.69 us
    ppermute x3, waiting for transfers between devices: 0.42 us -> 2.66 us  [body(): lax.ppermute(param, 'zl', shift(nz, k))]
    pallas_call x8 -> x10, Pallas kernels: 12.2 us -> 14 us  [call(): pl.pallas_call(kernel, out_shape=out, in_specs=specs, out_specs=out_specs...]
  transfers between devices with their start and end apart: 7 -> 7, of which waited for: 4 -> 5; matrix products, arithmetic and copies ran while one was open for 0% -> 0% of each run, Pallas kernels for 2% -> 5%
where the time goes in v3:
time: 107 us
  blocking collectives  60.4 us (56%)
  starting transfers between devices  19.4 us (18%)
  Pallas kernels  14 us (13%)
  waiting for transfers between devices  10.4 us (10%)
  local copies, waits for them, and re-layouts  2.69 us (3%)
    all_to_all x4, blocking collectives, exchange(): return lax.all_to_all(a, axes, split_axis=0, concat_axis=0, tiled=True)  60.4 us
    pallas_call x10, Pallas kernels, call(): pl.pallas_call(kernel, out_shape=out, in_specs=specs, out_specs=out_specs...  14 us
    ppermute x3, starting transfers between devices, swap_core(): return lax.ppermute(a, 'core', shift(2, 1))  12.5 us
    all_to_all x1, waiting for transfers between devices, exchange(): return lax.all_to_all(a, axes, split_axis=0, concat_axis=0, tiled=True)  4.62 us
    all_to_all x1, starting transfers between devices, exchange(): return lax.all_to_all(a, axes, split_axis=0, concat_axis=0, tiled=True)  3.96 us
    ppermute x3, waiting for transfers between devices, swap_core(): return lax.ppermute(a, 'core', shift(2, 1))  3.11 us
    ppermute x3, starting transfers between devices, body(): lax.ppermute(param, 'zl', shift(nz, k))  2.92 us
    unnamed x12, local copies, waits for them, and re-layouts  2.69 us
  transfers between devices with their start and end apart: 7, of which 5 were waited for; matrix products, arithmetic and copies ran while one was open for 0% of the time, Pallas kernels for 5%

profile of v3, /device:TPU:1, one launch (start us, length us, event | category | flops | bytes accessed | tf_op | source)
XLA Modules:
  0.0 107.0 jit_solution(4312752150934838230)
XLA Ops:
  0.0 3.2 %collective-permute-start = (bf16[512,2048]{1,0:T(8,128)(2,1)}, bf16[512,2048]{1,0:T(8,128)(2,1)S(1)}, u32[]{:S(2)}, u32[]{:S(2)}) collective-permute-start(bf16[512,2048]{1,0:T(8,128)(2,1)} %refs_1_.1), channel_id=1, source_target_pairs={{0,2},{2,0},{1,3},{3,1},{4,6},{6,4},{5,7},{7,5},{8,10},{10,8},{9,1... | collective-permute-start | bytes 6291464 | tf_op jit(solution)/shard_map/ppermute | solution.py:32
  3.2 2.6 %collective-permute-start.3 = (bf16[4,2048]{1,0:T(4,128)(2,1)}, bf16[4,2048]{1,0:T(4,128)(2,1)S(1)}, u32[]{:S(2)}, u32[]{:S(2)}) collective-permute-start(bf16[4,2048]{1,0:T(4,128)(2,1)} %bitcast.8), channel_id=1, source_target_pairs={{0,48},{16,0},{32,16},{48,32},{1,49},{17,1},{33,17},{49,33},{2,50}... | collective-permute-start | bytes 49160 | tf_op jit(solution)/shard_map/ppermute | solution.py:229
  5.9 0.0 collective-permute-start.2
  5.9 0.3 collective-permute-start.1
  6.2 1.6 %shard_map.46 = (bf16[4,2048]{1,0:T(4,128)(2,1)S(1)}, bf16[512,2048]{1,0:T(8,128)(2,1)S(1)}) custom-call(bf16[4,2048]{1,0:T(4,128)(2,1)} %bitcast.11, bf16[512,2048]{1,0:T(8,128)(2,1)} %refs_1_.1), custom_call_target="tpu_custom_call" | custom-call | flops 2147483648 | bytes 1048576 | tf_op jit(solution)/shard_map/pallas_call | solution.py:46
  7.8 0.0 collective-permute-done.3.refs_3_
  7.8 1.7 %collective-permute-done.2.refs_2_ = bf16[4,2048]{1,0:T(4,128)(2,1)S(1)} collective-permute-done((bf16[4,2048]{1,0:T(4,128)(2,1)}, bf16[4,2048]{1,0:T(4,128)(2,1)S(1)}, u32[]{:S(2)}, u32[]{:S(2)}) %collective-permute-start.2) | collective-permute-done | bytes 16416 | tf_op jit(solution)/shard_map/ppermute | solution.py:229
  9.6 0.9 collective-permute-done.1.refs_1_
  10.5 0.2 shard_map.47
  10.6 21.2 %all_to_all.25 = bf16[16,16,2048]{2,1,0:T(8,128)(2,1)S(1)} all-to-all(bf16[16,16,2048]{2,1,0:T(8,128)(2,1)S(1)} %shard_map.47), channel_id=1, replica_groups=mesh['x'=4,'zl'=4,'y'=4,'core'=2,'zh'=2] {'x','y'}, dimensions={0} | all-to-all | bytes 2097152 | tf_op jit(solution)/shard_map/all_to_all | solution.py:36
  31.9 0.0 collective-permute-done.tok_b
  31.9 3.5 %shard_map.48 = (bf16[256,2176]{1,0:T(8,128)(2,1)}, f32[256,512]{1,0:T(8,128)S(1)}, f32[256,512]{1,0:T(8,128)S(1)}) custom-call(bf16[512,2048]{1,0:T(8,128)(2,1)S(1)} %get-tuple-element.16.tok_a, bf16[512,2048]{1,0:T(8,128)(2,1)S(1)} %collective-permute-done.tok_b, bf16[256,2048]{1,0:T(8,128)(2,1)S(1)} %bitcast.7), custom_call_target="tpu_custom_call" | custom-call | flops 2147483648 | bytes 1048576 | tf_op jit(solution)/shard_map/pallas_call | solution.py:46
  35.3 4.0 %all-to-all-start.1 = ((bf16[16,16,2176]{2,1,0:T(8,128)(2,1)}), bf16[16,16,2176]{2,1,0:T(8,128)(2,1)S(1)}, u32[]{:S(2)}, u32[]{:S(2)}) async-start(bf16[16,16,2176]{2,1,0:T(8,128)(2,1)} %bitcast.3), calls=%async_computation.1 | async-start | bytes 2228224 | tf_op jit(solution)/shard_map/all_to_all | solution.py:36
  39.3 3.2 %collective-permute-start.4 = (f32[256,512]{1,0:T(8,128)S(1)}, f32[256,512]{1,0:T(8,128)S(1)}, u32[]{:S(2)}, u32[]{:S(2)}) collective-permute-start(f32[256,512]{1,0:T(8,128)S(1)} %get-tuple-element.19), channel_id=1, source_target_pairs={{0,2},{2,0},{1,3},{3,1},{4,6},{6,4},{5,7},{7,5},{8,10},{10,8},{9,1... | collective-permute-start | bytes 1572872 | tf_op jit(solution)/shard_map/ppermute | solution.py:32
  42.5 1.5 %collective-permute-done.4.log_c = f32[256,512]{1,0:T(8,128)S(1)} collective-permute-done((f32[256,512]{1,0:T(8,128)S(1)}, f32[256,512]{1,0:T(8,128)S(1)}, u32[]{:S(2)}, u32[]{:S(2)}) %collective-permute-start.4) | collective-permute-done | bytes 524320 | tf_op jit(solution)/shard_map/ppermute | solution.py:32
  44.0 0.5 shard_map.49
  44.5 0.0 copy-start.4
  44.5 0.7 copy-done.4
  45.2 2.2 %shard_map.50 = (bf16[512,1024]{1,0:T(8,128)(2,1)S(1)}, bf16[512,1024]{1,0:T(8,128)(2,1)S(1)}, bf16[512,1024]{1,0:T(8,128)(2,1)S(1)}, bf16[512,1024]{1,0:T(8,128)(2,1)S(1)}) custom-call(bf16[1,2048,1024]{2,1,0:T(8,128)(2,1)} %whole.1, bf16[512,256]{1,0:T(8,128)(2,1)S(1)} %get-tuple-element.20.after.weight), custom_call_target="tpu_custom_call" | custom-call | flops 2147483648 | bytes 1048576 | tf_op jit(solution)/shard_map/pallas_call | solution.py:46
  47.4 0.0 copy-start
  47.5 1.0 copy-done
  48.4 0.0 copy-start.2
  48.4 1.0 copy-done.2
  49.4 4.6 %all-to-all-done.1.got = bf16[16,16,2176]{2,1,0:T(8,128)(2,1)S(1)} async-done(((bf16[16,16,2176]{2,1,0:T(8,128)(2,1)}), bf16[16,16,2176]{2,1,0:T(8,128)(2,1)S(1)}, u32[]{:S(2)}, u32[]{:S(2)}) %all-to-all-start.1) | async-done | bytes 1114144 | tf_op jit(solution)/shard_map/all_to_all | solution.py:36
  54.1 0.0 copy-start.1
  54.1 0.0 copy-start.3
  54.1 0.4 shard_map.51
  54.4 12.4 %all_to_all.26.got = bf16[8,4,2176]{2,1,0:T(4,128)(2,1)S(1)} all-to-all(bf16[8,4,2176]{2,1,0:T(4,128)(2,1)S(1)} %shard_map.51), channel_id=1, replica_groups=mesh['x'=4,'zl'=4,'y'=4,'core'=2,'zh'=2] {'zl','zh'}, dimensions={0} | all-to-all | bytes 278528 | tf_op jit(solution)/shard_map/all_to_all | solution.py:36
  66.9 0.0 copy-done.1
  66.9 0.0 copy-done.3
  66.9 3.2 %shard_map.52 = bf16[8,4,2048]{2,1,0:T(4,128)(2,1)S(1)} custom-call(bf16[8,4,2176]{2,1,0:T(4,128)(2,1)S(1)} %all_to_all.26.got, bf16[512,1024]{1,0:T(8,128)(2,1)S(1)} %get-tuple-element.23.refs_0_, bf16[512,1024]{1,0:T(8,128)(2,1)S(1)} %copy-done.1, bf16[512,1024]{1,0:T(8,128)(2,1)S(1)} %copy-done.3, bf16[512,1024]{1,0:T(8,128)(2,1)S(1)} %get-tuple-element.22.after.refs_3_, ...), custom_call_target="tpu_custom_call" | custom-call | flops 33554432 | bytes 1048576 | tf_op jit(solution)/shard_map/pallas_call | solution.py:46
  70.1 9.4 %all_to_all.27.got = bf16[8,4,2048]{2,1,0:T(4,128)(2,1)S(1)} all-to-all(bf16[8,4,2048]{2,1,0:T(4,128)(2,1)S(1)} %shard_map.52), channel_id=1, replica_groups=mesh['x'=4,'zl'=4,'y'=4,'core'=2,'zh'=2] {'zl','zh'}, dimensions={0} | all-to-all | bytes 262144 | tf_op jit(solution)/shard_map/all_to_all | solution.py:36
  79.5 0.1 shard_map.53
  79.6 17.4 %all_to_all.28 = bf16[16,16,2048]{2,1,0:T(8,128)(2,1)S(1)} all-to-all(bf16[16,16,2048]{2,1,0:T(8,128)(2,1)S(1)} %shard_map.53), channel_id=1, replica_groups=mesh['x'=4,'zl'=4,'y'=4,'core'=2,'zh'=2] {'x','y'}, dimensions={0} | all-to-all | bytes 2097152 | tf_op jit(solution)/shard_map/all_to_all | solution.py:36
  97.0 0.0 copy-start.5
  97.0 6.1 %collective-permute-start.5 = (bf16[256,2048]{1,0:T(8,128)(2,1)S(1)}, bf16[256,2048]{1,0:T(8,128)(2,1)S(1)}, u32[]{:S(2)}, u32[]{:S(2)}) collective-permute-start(bf16[256,2048]{1,0:T(8,128)(2,1)S(1)} %bitcast.5), channel_id=1, source_target_pairs={{0,2},{2,0},{1,3},{3,1},{4,6},{6,4},{5,7},{7,5},{8,10},{10,8},{9,1... | collective-permute-start | bytes 3145736 | tf_op jit(solution)/shard_map/ppermute | solution.py:32
  103.0 0.7 shard_map.54.acc
  103.8 1.6 %collective-permute-done.5.rows = bf16[256,2048]{1,0:T(8,128)(2,1)S(1)} collective-permute-done((bf16[256,2048]{1,0:T(8,128)(2,1)S(1)}, bf16[256,2048]{1,0:T(8,128)(2,1)S(1)}, u32[]{:S(2)}, u32[]{:S(2)}) %collective-permute-start.5) | collective-permute-done | bytes 1048608 | tf_op jit(solution)/shard_map/ppermute | solution.py:32
  105.3 0.0 copy-done.5
  105.3 1.7 %shard_map.55 = bf16[512,2048]{1,0:T(8,128)(2,1)} custom-call(f32[512,2048]{1,0:T(8,128)S(1)} %shard_map.54.acc, bf16[512,256]{1,0:T(8,128)(2,1)S(1)} %copy-done.5, bf16[256,2048]{1,0:T(8,128)(2,1)S(1)} %collective-permute-done.5.rows), custom_call_target="tpu_custom_call" | custom-call | flops 536870912 | bytes 1048576 | tf_op jit(solution)/shard_map/pallas_call | solution.py:46
Async XLA Ops:
  0.0 31.9 %collective-permute-start = (bf16[512,2048]{1,0:T(8,128)(2,1)}, bf16[512,2048]{1,0:T(8,128)(2,1)S(1)}, u32[]{:S(2)}, u32[]{:S(2)}) collective-permute-start(bf16[512,2048]{1,0:T(8,128)(2,1)} %refs_1_.1), channel_id=1, source_target_pairs={{0,2},{2,0},{1,3},{3,1},{4,6},{6,4},{5,7},{7,5},{8,10},{10,8},{9,1... | collective-permute-start | bytes 6291464 | tf_op jit(solution)/shard_map/ppermute | solution.py:32
  3.2 4.6 %collective-permute-start.3 = (bf16[4,2048]{1,0:T(4,128)(2,1)}, bf16[4,2048]{1,0:T(4,128)(2,1)S(1)}, u32[]{:S(2)}, u32[]{:S(2)}) collective-permute-start(bf16[4,2048]{1,0:T(4,128)(2,1)} %bitcast.8), channel_id=1, source_target_pairs={{0,48},{16,0},{32,16},{48,32},{1,49},{17,1},{33,17},{49,33},{2,50}... | collective-permute-start | bytes 49160 | tf_op jit(solution)/shard_map/ppermute | solution.py:229
  5.9 3.7 %collective-permute-start.2 = (bf16[4,2048]{1,0:T(4,128)(2,1)}, bf16[4,2048]{1,0:T(4,128)(2,1)S(1)}, u32[]{:S(2)}, u32[]{:S(2)}) collective-permute-start(bf16[4,2048]{1,0:T(4,128)(2,1)} %bitcast.9), channel_id=1, source_target_pairs={{0,32},{16,48},{32,0},{48,16},{1,33},{17,49},{33,1},{49,17},{2,34}... | collective-permute-start | bytes 49160 | tf_op jit(solution)/shard_map/ppermute | solution.py:229
  5.9 4.6 %collective-permute-start.1 = (bf16[4,2048]{1,0:T(4,128)(2,1)}, bf16[4,2048]{1,0:T(4,128)(2,1)S(1)}, u32[]{:S(2)}, u32[]{:S(2)}) collective-permute-start(bf16[4,2048]{1,0:T(4,128)(2,1)} %bitcast.10), channel_id=1, source_target_pairs={{0,16},{16,32},{32,48},{48,0},{1,17},{17,33},{33,49},{49,1},{2,18}... | collective-permute-start | bytes 49160 | tf_op jit(solution)/shard_map/ppermute | solution.py:229
  35.3 18.7 %all-to-all-start.1 = ((bf16[16,16,2176]{2,1,0:T(8,128)(2,1)}), bf16[16,16,2176]{2,1,0:T(8,128)(2,1)S(1)}, u32[]{:S(2)}, u32[]{:S(2)}) async-start(bf16[16,16,2176]{2,1,0:T(8,128)(2,1)} %bitcast.3), calls=%async_computation.1 | async-start | bytes 2228224 | tf_op jit(solution)/shard_map/all_to_all | solution.py:36
  39.3 4.8 %collective-permute-start.4 = (f32[256,512]{1,0:T(8,128)S(1)}, f32[256,512]{1,0:T(8,128)S(1)}, u32[]{:S(2)}, u32[]{:S(2)}) collective-permute-start(f32[256,512]{1,0:T(8,128)S(1)} %get-tuple-element.19), channel_id=1, source_target_pairs={{0,2},{2,0},{1,3},{3,1},{4,6},{6,4},{5,7},{7,5},{8,10},{10,8},{9,1... | collective-permute-start | bytes 1572872 | tf_op jit(solution)/shard_map/ppermute | solution.py:32
  44.5 0.7 copy-start.4
  47.4 1.0 copy-start
  48.4 1.0 copy-start.2
  54.1 12.8 %copy-start.1 = (bf16[512,1024]{1,0:T(8,128)(2,1)S(1)}, bf16[512,1024]{1,0:T(8,128)(2,1)}, u32[]{:S(2)}) copy-start(bf16[512,1024]{1,0:T(8,128)(2,1)} %copy-done) | copy-start | bytes 3145732
  54.1 12.8 %copy-start.3 = (bf16[512,1024]{1,0:T(8,128)(2,1)S(1)}, bf16[512,1024]{1,0:T(8,128)(2,1)}, u32[]{:S(2)}) copy-start(bf16[512,1024]{1,0:T(8,128)(2,1)} %copy-done.2) | copy-start | bytes 3145732
  97.0 8.3 %copy-start.5 = (bf16[512,256]{1,0:T(8,128)(2,1)S(1)}, bf16[512,256]{1,0:T(8,128)(2,1)}, u32[]{:S(2)}) copy-start(bf16[512,256]{1,0:T(8,128)(2,1)} %copy-done.4) | copy-start | bytes 786436
  97.0 8.3 %collective-permute-start.5 = (bf16[256,2048]{1,0:T(8,128)(2,1)S(1)}, bf16[256,2048]{1,0:T(8,128)(2,1)S(1)}, u32[]{:S(2)}, u32[]{:S(2)}) collective-permute-start(bf16[256,2048]{1,0:T(8,128)(2,1)S(1)} %bitcast.5), channel_id=1, source_target_pairs={{0,2},{2,0},{1,3},{3,1},{4,6},{6,4},{5,7},{7,5},{8,10},{10,8},{9,1... | collective-permute-start | bytes 3145736 | tf_op jit(solution)/shard_map/ppermute | solution.py:32

commit v4 on v3

--- a/solution.py
+++ b/solution.py
@@ -91,7 +91,7 @@
         c.wait()
 
 
-def slots_kernel(tok_a, tok_b, hat, sent, log_a, log_b):
+def slots_kernel(tok_a, tok_b, hat, sent, log_a, log_b, held, sems):
     d = tok_a.shape[1]
     parts = []
     for tok, out in ((tok_b, log_b), (tok_a, log_a)):
@@ -102,11 +102,18 @@
         parts.append((tok, terms.astype(jnp.bfloat16), peak, jnp.sum(terms, axis=1, keepdims=True)))
     peak = jnp.maximum(parts[0][2], parts[1][2])
     scale = [jnp.exp(p[2] - peak) for p in parts]
-    sent[:, d:] = tail_of(peak, sum(p[3] * s for p, s in zip(parts, scale)))
-    for j in range(0, d, SUM_TILE):
-        cols = slice(j, j + SUM_TILE)
+    held[:, d:] = tail_of(peak, sum(p[3] * s for p, s in zip(parts, scale)))
+    copies = [pltpu.make_async_copy(held.at[:, pl.ds(d, PAD)], sent.at[:, pl.ds(d, PAD)], sems.at[0])]
+    copies[0].start()
+    for i in range(d // SUM_TILE):
+        cols = slice(i * SUM_TILE, (i + 1) * SUM_TILE)
         sums = [jnp.dot(p[1], p[0][:, cols], preferred_element_type=jnp.float32) * s for p, s in zip(parts, scale)]
-        sent[:, cols] = (sums[0] + sums[1]).astype(jnp.bfloat16)
+        held[:, cols] = (sums[0] + sums[1]).astype(jnp.bfloat16)
+        place = pl.ds(i * SUM_TILE, SUM_TILE)
+        copies.append(pltpu.make_async_copy(held.at[:, place], sent.at[:, place], sems.at[i + 1]))
+        copies[-1].start()
+    for c in copies:
+        c.wait()
 
 
 def weights_of(tails):
@@ -234,6 +241,7 @@
             slots_kernel,
             [S((own, d + PAD), bf), S((own, n_tok), f32), S((own, n_tok), f32)],
             tokens_a, tokens_b, hat.reshape(own, d), flops=8 * own * n_tok * d,
+            out_specs=[ANY, VMEM, VMEM], scratch=[pltpu.VMEM((own, d + PAD), bf), DMA((d // SUM_TILE + 1,))],
         )
         got = exchange(sent.reshape(plane, rows, d + PAD), PLANE)
         log_c = swap_core(log_b)

time: 107 us -> 107 us (level)
  no operation moved by 1% of the time
where the time goes in v4:
time: 107 us
  blocking collectives  60.4 us (56%)
  starting transfers between devices  19.4 us (18%)
  Pallas kernels  13.8 us (13%)
  waiting for transfers between devices  10.4 us (10%)
  local copies, waits for them, and re-layouts  2.69 us (3%)
    all_to_all x4, blocking collectives, exchange(): return lax.all_to_all(a, axes, split_axis=0, concat_axis=0, tiled=True)  60.4 us
    pallas_call x10, Pallas kernels, call(): pl.pallas_call(kernel, out_shape=out, in_specs=specs, out_specs=out_specs...  13.8 us
    ppermute x3, starting transfers between devices, swap_core(): return lax.ppermute(a, 'core', shift(2, 1))  12.5 us
    all_to_all x1, waiting for transfers between devices, exchange(): return lax.all_to_all(a, axes, split_axis=0, concat_axis=0, tiled=True)  4.63 us
    all_to_all x1, starting transfers between devices, exchange(): return lax.all_to_all(a, axes, split_axis=0, concat_axis=0, tiled=True)  3.98 us
    ppermute x3, waiting for transfers between devices, swap_core(): return lax.ppermute(a, 'core', shift(2, 1))  3.11 us
    ppermute x3, starting transfers between devices, body(): lax.ppermute(param, 'zl', shift(nz, k))  2.92 us
    unnamed x12, local copies, waits for them, and re-layouts  2.69 us
  transfers between devices with their start and end apart: 7, of which 5 were waited for; matrix products, arithmetic and copies ran while one was open for 0% of the time, Pallas kernels for 5%

profile of v4, /device:TPU:1, one launch (start us, length us, event | category | flops | bytes accessed | tf_op | source)
XLA Modules:
  0.0 106.8 jit_solution(13052500166317896664)
XLA Ops:
  0.0 3.2 %collective-permute-start = (bf16[512,2048]{1,0:T(8,128)(2,1)}, bf16[512,2048]{1,0:T(8,128)(2,1)S(1)}, u32[]{:S(2)}, u32[]{:S(2)}) collective-permute-start(bf16[512,2048]{1,0:T(8,128)(2,1)} %refs_1_.1), channel_id=1, source_target_pairs={{0,2},{2,0},{1,3},{3,1},{4,6},{6,4},{5,7},{7,5},{8,10},{10,8},{9,1... | collective-permute-start | bytes 6291464 | tf_op jit(solution)/shard_map/ppermute | solution.py:32
  3.2 2.6 %collective-permute-start.3 = (bf16[4,2048]{1,0:T(4,128)(2,1)}, bf16[4,2048]{1,0:T(4,128)(2,1)S(1)}, u32[]{:S(2)}, u32[]{:S(2)}) collective-permute-start(bf16[4,2048]{1,0:T(4,128)(2,1)} %bitcast.8), channel_id=1, source_target_pairs={{0,48},{16,0},{32,16},{48,32},{1,49},{17,1},{33,17},{49,33},{2,50}... | collective-permute-start | bytes 49160 | tf_op jit(solution)/shard_map/ppermute | solution.py:236
  5.9 0.0 collective-permute-start.2
  5.9 0.3 collective-permute-start.1
  6.2 1.6 %shard_map.46 = (bf16[4,2048]{1,0:T(4,128)(2,1)S(1)}, bf16[512,2048]{1,0:T(8,128)(2,1)S(1)}) custom-call(bf16[4,2048]{1,0:T(4,128)(2,1)} %bitcast.11, bf16[512,2048]{1,0:T(8,128)(2,1)} %refs_1_.1), custom_call_target="tpu_custom_call" | custom-call | flops 2147483648 | bytes 1048576 | tf_op jit(solution)/shard_map/pallas_call | solution.py:46
  7.8 0.0 collective-permute-done.3.refs_3_
  7.8 1.7 %collective-permute-done.2.refs_2_ = bf16[4,2048]{1,0:T(4,128)(2,1)S(1)} collective-permute-done((bf16[4,2048]{1,0:T(4,128)(2,1)}, bf16[4,2048]{1,0:T(4,128)(2,1)S(1)}, u32[]{:S(2)}, u32[]{:S(2)}) %collective-permute-start.2) | collective-permute-done | bytes 16416 | tf_op jit(solution)/shard_map/ppermute | solution.py:236
  9.6 0.9 collective-permute-done.1.refs_1_
  10.5 0.2 shard_map.47
  10.6 21.2 %all_to_all.25 = bf16[16,16,2048]{2,1,0:T(8,128)(2,1)S(1)} all-to-all(bf16[16,16,2048]{2,1,0:T(8,128)(2,1)S(1)} %shard_map.47), channel_id=1, replica_groups=mesh['x'=4,'zl'=4,'y'=4,'core'=2,'zh'=2] {'x','y'}, dimensions={0} | all-to-all | bytes 2097152 | tf_op jit(solution)/shard_map/all_to_all | solution.py:36
  31.9 0.0 collective-permute-done.tok_b
  31.9 3.3 %shard_map.48 = (bf16[256,2176]{1,0:T(8,128)(2,1)}, f32[256,512]{1,0:T(8,128)S(1)}, f32[256,512]{1,0:T(8,128)S(1)}) custom-call(bf16[512,2048]{1,0:T(8,128)(2,1)S(1)} %get-tuple-element.16.tok_a, bf16[512,2048]{1,0:T(8,128)(2,1)S(1)} %collective-permute-done.tok_b, bf16[256,2048]{1,0:T(8,128)(2,1)S(1)} %bitcast.7), custom_call_target="tpu_custom_call" | custom-call | flops 2147483648 | bytes 1048576 | tf_op jit(solution)/shard_map/pallas_call | solution.py:46
  35.1 4.0 %all-to-all-start.1 = ((bf16[16,16,2176]{2,1,0:T(8,128)(2,1)}), bf16[16,16,2176]{2,1,0:T(8,128)(2,1)S(1)}, u32[]{:S(2)}, u32[]{:S(2)}) async-start(bf16[16,16,2176]{2,1,0:T(8,128)(2,1)} %bitcast.3), calls=%async_computation.1 | async-start | bytes 2228224 | tf_op jit(solution)/shard_map/all_to_all | solution.py:36
  39.1 3.2 %collective-permute-start.4 = (f32[256,512]{1,0:T(8,128)S(1)}, f32[256,512]{1,0:T(8,128)S(1)}, u32[]{:S(2)}, u32[]{:S(2)}) collective-permute-start(f32[256,512]{1,0:T(8,128)S(1)} %get-tuple-element.19), channel_id=1, source_target_pairs={{0,2},{2,0},{1,3},{3,1},{4,6},{6,4},{5,7},{7,5},{8,10},{10,8},{9,1... | collective-permute-start | bytes 1572872 | tf_op jit(solution)/shard_map/ppermute | solution.py:32
  42.4 1.5 %collective-permute-done.4.log_c = f32[256,512]{1,0:T(8,128)S(1)} collective-permute-done((f32[256,512]{1,0:T(8,128)S(1)}, f32[256,512]{1,0:T(8,128)S(1)}, u32[]{:S(2)}, u32[]{:S(2)}) %collective-permute-start.4) | collective-permute-done | bytes 524320 | tf_op jit(solution)/shard_map/ppermute | solution.py:32
  43.9 0.5 shard_map.49
  44.4 0.0 copy-start.4
  44.4 0.7 copy-done.4
  45.1 2.2 %shard_map.50 = (bf16[512,1024]{1,0:T(8,128)(2,1)S(1)}, bf16[512,1024]{1,0:T(8,128)(2,1)S(1)}, bf16[512,1024]{1,0:T(8,128)(2,1)S(1)}, bf16[512,1024]{1,0:T(8,128)(2,1)S(1)}) custom-call(bf16[1,2048,1024]{2,1,0:T(8,128)(2,1)} %whole.1, bf16[512,256]{1,0:T(8,128)(2,1)S(1)} %get-tuple-element.20.after.weight), custom_call_target="tpu_custom_call" | custom-call | flops 2147483648 | bytes 1048576 | tf_op jit(solution)/shard_map/pallas_call | solution.py:46
  47.3 0.0 copy-start
  47.3 1.0 copy-done
  48.3 0.0 copy-start.2
  48.3 1.0 copy-done.2
  49.3 4.6 %all-to-all-done.1.got = bf16[16,16,2176]{2,1,0:T(8,128)(2,1)S(1)} async-done(((bf16[16,16,2176]{2,1,0:T(8,128)(2,1)}), bf16[16,16,2176]{2,1,0:T(8,128)(2,1)S(1)}, u32[]{:S(2)}, u32[]{:S(2)}) %all-to-all-start.1) | async-done | bytes 1114144 | tf_op jit(solution)/shard_map/all_to_all | solution.py:36
  53.9 0.0 copy-start.1
  53.9 0.0 copy-start.3
  53.9 0.4 shard_map.51
  54.3 12.4 %all_to_all.26.got = bf16[8,4,2176]{2,1,0:T(4,128)(2,1)S(1)} all-to-all(bf16[8,4,2176]{2,1,0:T(4,128)(2,1)S(1)} %shard_map.51), channel_id=1, replica_groups=mesh['x'=4,'zl'=4,'y'=4,'core'=2,'zh'=2] {'zl','zh'}, dimensions={0} | all-to-all | bytes 278528 | tf_op jit(solution)/shard_map/all_to_all | solution.py:36
  66.7 0.0 copy-done.1
  66.7 0.0 copy-done.3
  66.7 3.2 %shard_map.52 = bf16[8,4,2048]{2,1,0:T(4,128)(2,1)S(1)} custom-call(bf16[8,4,2176]{2,1,0:T(4,128)(2,1)S(1)} %all_to_all.26.got, bf16[512,1024]{1,0:T(8,128)(2,1)S(1)} %get-tuple-element.23.refs_0_, bf16[512,1024]{1,0:T(8,128)(2,1)S(1)} %copy-done.1, bf16[512,1024]{1,0:T(8,128)(2,1)S(1)} %copy-done.3, bf16[512,1024]{1,0:T(8,128)(2,1)S(1)} %get-tuple-element.22.after.refs_3_, ...), custom_call_target="tpu_custom_call" | custom-call | flops 33554432 | bytes 1048576 | tf_op jit(solution)/shard_map/pallas_call | solution.py:46
  70.0 9.4 %all_to_all.27.got = bf16[8,4,2048]{2,1,0:T(4,128)(2,1)S(1)} all-to-all(bf16[8,4,2048]{2,1,0:T(4,128)(2,1)S(1)} %shard_map.52), channel_id=1, replica_groups=mesh['x'=4,'zl'=4,'y'=4,'core'=2,'zh'=2] {'zl','zh'}, dimensions={0} | all-to-all | bytes 262144 | tf_op jit(solution)/shard_map/all_to_all | solution.py:36
  79.3 0.1 shard_map.53
  79.5 17.4 %all_to_all.28 = bf16[16,16,2048]{2,1,0:T(8,128)(2,1)S(1)} all-to-all(bf16[16,16,2048]{2,1,0:T(8,128)(2,1)S(1)} %shard_map.53), channel_id=1, replica_groups=mesh['x'=4,'zl'=4,'y'=4,'core'=2,'zh'=2] {'x','y'}, dimensions={0} | all-to-all | bytes 2097152 | tf_op jit(solution)/shard_map/all_to_all | solution.py:36
  96.8 0.0 copy-start.5
  96.8 6.1 %collective-permute-start.5 = (bf16[256,2048]{1,0:T(8,128)(2,1)S(1)}, bf16[256,2048]{1,0:T(8,128)(2,1)S(1)}, u32[]{:S(2)}, u32[]{:S(2)}) collective-permute-start(bf16[256,2048]{1,0:T(8,128)(2,1)S(1)} %bitcast.5), channel_id=1, source_target_pairs={{0,2},{2,0},{1,3},{3,1},{4,6},{6,4},{5,7},{7,5},{8,10},{10,8},{9,1... | collective-permute-start | bytes 3145736 | tf_op jit(solution)/shard_map/ppermute | solution.py:32
  102.9 0.7 shard_map.54.acc
  103.6 1.6 %collective-permute-done.5.rows = bf16[256,2048]{1,0:T(8,128)(2,1)S(1)} collective-permute-done((bf16[256,2048]{1,0:T(8,128)(2,1)S(1)}, bf16[256,2048]{1,0:T(8,128)(2,1)S(1)}, u32[]{:S(2)}, u32[]{:S(2)}) %collective-permute-start.5) | collective-permute-done | bytes 1048608 | tf_op jit(solution)/shard_map/ppermute | solution.py:32
  105.2 0.0 copy-done.5
  105.2 1.7 %shard_map.55 = bf16[512,2048]{1,0:T(8,128)(2,1)} custom-call(f32[512,2048]{1,0:T(8,128)S(1)} %shard_map.54.acc, bf16[512,256]{1,0:T(8,128)(2,1)S(1)} %copy-done.5, bf16[256,2048]{1,0:T(8,128)(2,1)S(1)} %collective-permute-done.5.rows), custom_call_target="tpu_custom_call" | custom-call | flops 536870912 | bytes 1048576 | tf_op jit(solution)/shard_map/pallas_call | solution.py:46
Async XLA Ops:
  0.0 31.9 %collective-permute-start = (bf16[512,2048]{1,0:T(8,128)(2,1)}, bf16[512,2048]{1,0:T(8,128)(2,1)S(1)}, u32[]{:S(2)}, u32[]{:S(2)}) collective-permute-start(bf16[512,2048]{1,0:T(8,128)(2,1)} %refs_1_.1), channel_id=1, source_target_pairs={{0,2},{2,0},{1,3},{3,1},{4,6},{6,4},{5,7},{7,5},{8,10},{10,8},{9,1... | collective-permute-start | bytes 6291464 | tf_op jit(solution)/shard_map/ppermute | solution.py:32
  3.2 4.6 %collective-permute-start.3 = (bf16[4,2048]{1,0:T(4,128)(2,1)}, bf16[4,2048]{1,0:T(4,128)(2,1)S(1)}, u32[]{:S(2)}, u32[]{:S(2)}) collective-permute-start(bf16[4,2048]{1,0:T(4,128)(2,1)} %bitcast.8), channel_id=1, source_target_pairs={{0,48},{16,0},{32,16},{48,32},{1,49},{17,1},{33,17},{49,33},{2,50}... | collective-permute-start | bytes 49160 | tf_op jit(solution)/shard_map/ppermute | solution.py:236
  5.9 3.7 %collective-permute-start.2 = (bf16[4,2048]{1,0:T(4,128)(2,1)}, bf16[4,2048]{1,0:T(4,128)(2,1)S(1)}, u32[]{:S(2)}, u32[]{:S(2)}) collective-permute-start(bf16[4,2048]{1,0:T(4,128)(2,1)} %bitcast.9), channel_id=1, source_target_pairs={{0,32},{16,48},{32,0},{48,16},{1,33},{17,49},{33,1},{49,17},{2,34}... | collective-permute-start | bytes 49160 | tf_op jit(solution)/shard_map/ppermute | solution.py:236
  5.9 4.6 %collective-permute-start.1 = (bf16[4,2048]{1,0:T(4,128)(2,1)}, bf16[4,2048]{1,0:T(4,128)(2,1)S(1)}, u32[]{:S(2)}, u32[]{:S(2)}) collective-permute-start(bf16[4,2048]{1,0:T(4,128)(2,1)} %bitcast.10), channel_id=1, source_target_pairs={{0,16},{16,32},{32,48},{48,0},{1,17},{17,33},{33,49},{49,1},{2,18}... | collective-permute-start | bytes 49160 | tf_op jit(solution)/shard_map/ppermute | solution.py:236
  35.1 18.8 %all-to-all-start.1 = ((bf16[16,16,2176]{2,1,0:T(8,128)(2,1)}), bf16[16,16,2176]{2,1,0:T(8,128)(2,1)S(1)}, u32[]{:S(2)}, u32[]{:S(2)}) async-start(bf16[16,16,2176]{2,1,0:T(8,128)(2,1)} %bitcast.3), calls=%async_computation.1 | async-start | bytes 2228224 | tf_op jit(solution)/shard_map/all_to_all | solution.py:36
  39.1 4.8 %collective-permute-start.4 = (f32[256,512]{1,0:T(8,128)S(1)}, f32[256,512]{1,0:T(8,128)S(1)}, u32[]{:S(2)}, u32[]{:S(2)}) collective-permute-start(f32[256,512]{1,0:T(8,128)S(1)} %get-tuple-element.19), channel_id=1, source_target_pairs={{0,2},{2,0},{1,3},{3,1},{4,6},{6,4},{5,7},{7,5},{8,10},{10,8},{9,1... | collective-permute-start | bytes 1572872 | tf_op jit(solution)/shard_map/ppermute | solution.py:32
  44.4 0.7 copy-start.4
  47.3 1.0 copy-start
  48.3 1.0 copy-start.2
  53.9 12.8 %copy-start.1 = (bf16[512,1024]{1,0:T(8,128)(2,1)S(1)}, bf16[512,1024]{1,0:T(8,128)(2,1)}, u32[]{:S(2)}) copy-start(bf16[512,1024]{1,0:T(8,128)(2,1)} %copy-done) | copy-start | bytes 3145732
  53.9 12.8 %copy-start.3 = (bf16[512,1024]{1,0:T(8,128)(2,1)S(1)}, bf16[512,1024]{1,0:T(8,128)(2,1)}, u32[]{:S(2)}) copy-start(bf16[512,1024]{1,0:T(8,128)(2,1)} %copy-done.2) | copy-start | bytes 3145732
  96.8 8.3 %copy-start.5 = (bf16[512,256]{1,0:T(8,128)(2,1)S(1)}, bf16[512,256]{1,0:T(8,128)(2,1)}, u32[]{:S(2)}) copy-start(bf16[512,256]{1,0:T(8,128)(2,1)} %copy-done.4) | copy-start | bytes 786436
  96.8 8.3 %collective-permute-start.5 = (bf16[256,2048]{1,0:T(8,128)(2,1)S(1)}, bf16[256,2048]{1,0:T(8,128)(2,1)S(1)}, u32[]{:S(2)}, u32[]{:S(2)}) collective-permute-start(bf16[256,2048]{1,0:T(8,128)(2,1)S(1)} %bitcast.5), channel_id=1, source_target_pairs={{0,2},{2,0},{1,3},{3,1},{4,6},{6,4},{5,7},{7,5},{8,10},{10,8},{9,1... | collective-permute-start | bytes 3145736 | tf_op jit(solution)/shard_map/ppermute | solution.py:32
